TPU v7x, 128 devices: a whole 4x4x4 slice. The times are simulated.
128 devices in a mesh: row: 4 (over z), ctx: 4 (over y_lo, core), head: 8 (over y_hi, x).
Axes of the slice: x: 4, y: 4 (y_hi: 2, y_lo: 2; y = y_hi * 2 + y_lo), z: 4, core: 2. Of those that a mesh axis runs over, the one named last changes fastest.
Arguments:
- tokens: bfloat16 [4, 4096, 1536], P('row', ('ctx', 'head')), may hold values from -6 to 6
- doc_lengths: int32 [4, 8], P('row'), may hold values from 1 to 3392, as said below
- w_query: bfloat16 [1536, 1536], P(('row', 'ctx')), may hold values from -0.15625 to 0.15625
- w_key: bfloat16 [1536, 768], P(('row', 'ctx')), may hold values from -0.15625 to 0.15625
- w_value: bfloat16 [1536, 768], P(('row', 'ctx')), may hold values from -0.15625 to 0.15625
- w_output: bfloat16 [1536, 1536], P(('row', 'ctx')), may hold values from -2.5 to 2.5
- w_gate: bfloat16 [1536, 4096], P(('row', 'ctx')), may hold values from -0.15625 to 0.15625
- w_up: bfloat16 [1536, 4096], P(('row', 'ctx')), may hold values from -0.15625 to 0.15625
- w_down: bfloat16 [4096, 1536], P(('row', 'ctx')), may hold values from -0.09375 to 0.09375
- gain_attn: bfloat16 [1536], P(('row', 'ctx')), may hold values from 0.25 to 1.75
- gain_mlp: bfloat16 [1536], P(('row', 'ctx')), may hold values from 0.25 to 1.75
- cotangent: bfloat16 [4, 4096, 1536], P('row', ('ctx', 'head')), may hold values from -6 to 6
Outputs:
- layer_out: bfloat16 [4, 4096, 1536], P('row', ('ctx', 'head'))
- tokens_grad: bfloat16 [4, 4096, 1536], P('row', ('ctx', 'head'))
- grad_query: float32 [1536, 1536], P(('row', 'ctx'))
- grad_key: float32 [1536, 768], P(('row', 'ctx'))
- grad_value: float32 [1536, 768], P(('row', 'ctx'))
- grad_output: float32 [1536, 1536], P(('row', 'ctx'))
- grad_gate: float32 [1536, 4096], P(('row', 'ctx'))
- grad_up: float32 [1536, 4096], P(('row', 'ctx'))
- grad_down: float32 [4096, 1536], P(('row', 'ctx'))
- grad_gain_attn: float32 [1536], P(('row', 'ctx'))
- grad_gain_mlp: float32 [1536], P(('row', 'ctx'))
Inputs may be any that keep to these rules, and one draw needn't show every extreme that they name: `doc_lengths`: each row's 8 document lengths, in order from position 0; their sum is less than 4096, and the positions after it are padding. In every row one document has the largest length and another has length 1.
All inputs are finite; a program needn't handle non-finite values.
Results may differ from a plain program's by a relative error of at most 0.025.
Values may be sent and summed in bfloat16 or wider, within the bound.
A program may use at most 256 MiB of HBM per device.

v0:
```python
from functools import partial

import jax
import jax.numpy as jnp
import numpy as np
from jax import lax
from jax.sharding import PartitionSpec as P

HEADS = 16
KV = 8
HD = 96


NORM_EPS = 1e-05


def frequency_table(head_width):
    halfway = head_width // 2
    base_freq = 500000.0 ** (-np.arange(halfway) * 2.0 / head_width)
    wavelength = 2.0 * np.pi / base_freq
    smooth = (8192.0 / wavelength - 1.0) / 3.0
    middle = (1.0 - smooth) * base_freq / 32.0 + smooth * base_freq
    freq_table = np.where(
        wavelength > 8192.0, base_freq / 32.0, np.where(wavelength < 2048.0, base_freq, middle)
    )
    return freq_table.astype(np.float32)


def doc_layout(lengths, places):
    doc_count = lengths.shape[0]
    doc_ends = jnp.cumsum(lengths)
    starts = doc_ends - lengths
    segment = jnp.sum((places[:, None] >= doc_ends[None, :]).astype(jnp.int32), axis=1)
    chosen = segment[:, None] == jnp.arange(doc_count, dtype=jnp.int32)[None, :]
    offset = jnp.sum(jnp.where(chosen, starts[None, :], 0), axis=1) + jnp.where(
        segment == doc_count, doc_ends[doc_count - 1], 0
    )
    return (segment, places - offset)


def rope_angles(offsets):
    frequency = jnp.asarray(frequency_table(HD))
    angles = offsets.astype(jnp.float32)[:, None] * frequency[None, :]
    return (jnp.cos(angles), jnp.sin(angles))


def rotate(vectors, cosine, sine_part):
    halfway = vectors.shape[-1] // 2
    first_half = vectors[..., :halfway]
    second = vectors[..., halfway:]
    cos_b = cosine[:, None, :]
    sin_b = sine_part[:, None, :]
    return jnp.concatenate(
        [first_half * cos_b - second * sin_b, second * cos_b + first_half * sin_b], axis=-1
    )


def matmul(left_side, right_side):
    return jnp.dot(left_side, right_side, preferred_element_type=jnp.float32)


def matmul_nt(left_side, right_side):
    return lax.dot_general(
        left_side, right_side, (((1,), (1,)), ((), ())), preferred_element_type=jnp.float32
    )


def matmul_tn(left_side, right_side):
    return lax.dot_general(
        left_side, right_side, (((0,), (0,)), ((), ())), preferred_element_type=jnp.float32
    )


def body(
    tokens,
    doc_lengths,
    w_query,
    w_key,
    w_value,
    w_output,
    w_gate,
    w_up,
    w_down,
    gain_attn,
    gain_mlp,
    cotangent,
):
    n_ctx = lax.axis_size("ctx")
    n_head = lax.axis_size("head")
    tok_count = tokens.shape[1]
    model_width = tokens.shape[2]
    kv_width = w_key.shape[1]
    hidden_width = w_gate.shape[1]
    group_size = HEADS // KV
    local_groups = KV // n_head
    local_heads = HEADS // n_head
    block_rows = tok_count * n_head
    score_scale = HD ** (-0.5)
    lengths = doc_lengths[0]
    doc_count = lengths.shape[0]
    ctx_index = lax.axis_index("ctx")
    head_index = lax.axis_index("head")
    own_places = (ctx_index * n_head + head_index) * tok_count + jnp.arange(
        tok_count, dtype=jnp.int32
    )
    own_segment, own_offsets = doc_layout(lengths, own_places)
    own_cosine, own_sine = rope_angles(own_offsets)
    inputs = tokens[0].astype(jnp.float32)
    recip_attn = lax.rsqrt(jnp.mean(inputs * inputs, axis=1, keepdims=True) + NORM_EPS)
    norm_attn = inputs * recip_attn
    piece_q = lax.all_gather(w_query, ("row", "ctx"), axis=0, tiled=True)
    piece_k = lax.all_gather(w_key, ("row", "ctx"), axis=0, tiled=True)
    piece_v = lax.all_gather(w_value, ("row", "ctx"), axis=0, tiled=True)
    piece_g = lax.all_gather(gain_attn, ("row", "ctx"), axis=0, tiled=True)
    normed = norm_attn * piece_g.astype(jnp.float32)[None, :]
    normed = normed.astype(jnp.bfloat16)
    queries = matmul(normed, piece_q)
    key_proj = matmul(normed, piece_k)
    value_proj = matmul(normed, piece_v)
    queries, key_proj, value_proj, h_attn = (queries, key_proj, value_proj, normed)
    query_rot = (
        rotate(queries.reshape(tok_count, HEADS, HD), own_cosine, own_sine)
        .astype(jnp.bfloat16)
        .reshape(tok_count, model_width)
    )
    key_rot = rotate(key_proj.reshape(tok_count, KV, HD), own_cosine, own_sine).astype(jnp.bfloat16)
    value_low = value_proj.reshape(tok_count, KV, HD).astype(jnp.bfloat16)
    packed = jnp.stack([key_rot, value_low], axis=2).reshape(tok_count, KV * 2 * HD)
    head_q, head_kv = (
        lax.all_to_all(query_rot, "head", split_axis=1, concat_axis=0, tiled=True),
        lax.all_to_all(packed, "head", split_axis=1, concat_axis=0, tiled=True),
    )
    q_places = ctx_index * block_rows + jnp.arange(block_rows, dtype=jnp.int32)
    q_segment, q_offsets = doc_layout(lengths, q_places)
    q_cosine, q_sine = rope_angles(q_offsets)
    q_valid = (q_segment < doc_count).astype(jnp.float32)
    q_blocks = head_q.reshape(block_rows, local_groups, group_size, HD)

    def block_mask(key_start):
        key_places = key_start + jnp.arange(block_rows, dtype=jnp.int32)
        key_segment, key_offsets = doc_layout(lengths, key_places)
        return (q_segment[:, None] == key_segment[None, :]) & (
            key_places[None, :] <= q_places[:, None]
        )

    def block_scores(block, key_start):
        scores = (
            jnp.einsum(
                "qgpd,kgd->gpqk", q_blocks, block[:, :, 0], preferred_element_type=jnp.float32
            )
            * score_scale
        )
        return jnp.where(block_mask(key_start)[None, None], scores, -jnp.inf)

    def attend_block(carry, block, key_start):
        accum, running, totals = carry
        scores = block_scores(block, key_start)
        new_top = jnp.maximum(running, jnp.max(scores, axis=3))
        factor = jnp.exp(running - new_top)
        weights = jnp.exp(scores - new_top[..., None])
        totals = totals * factor + jnp.sum(weights, axis=3)
        accum = accum * factor[..., None] + jnp.einsum(
            "gpqk,kgd->gpqd",
            weights.astype(jnp.bfloat16),
            block[:, :, 1],
            preferred_element_type=jnp.float32,
        )
        return (accum, new_top, totals)

    def over_blocks(step_fn, carry, piece, start):
        for number in range(piece.shape[0] // block_rows):
            key_start = start + number * block_rows
            block = piece[number * block_rows : (number + 1) * block_rows].reshape(
                block_rows, local_groups, 2, HD
            )
            carry = lax.cond(
                key_start <= ctx_index * block_rows,
                partial(step_fn, block=block, key_start=key_start),
                lambda kept: kept,
                carry,
            )
        return carry

    stat_shape = (local_groups, group_size, block_rows)
    start_attn = (
        jnp.zeros(stat_shape + (HD,), jnp.float32),
        jnp.full(stat_shape, -1e30, jnp.float32),
        jnp.zeros(stat_shape, jnp.float32),
    )
    accum, running, totals = over_blocks(
        attend_block, start_attn, lax.all_gather(head_kv, "ctx", axis=0, tiled=True), jnp.int32(0)
    )
    attn_heads = accum / totals[..., None]
    log_total = running + jnp.log(totals)
    masked = attn_heads * q_valid[None, None, :, None]
    head_out = (
        masked.transpose(2, 0, 1, 3).reshape(block_rows, local_heads * HD).astype(jnp.bfloat16)
    )
    attn_tok = lax.all_to_all(head_out, "head", split_axis=0, concat_axis=1, tiled=True)
    full_o, full_g2, full_gate, full_up, full_down = (
        lax.all_gather(w_output, ("row", "ctx"), axis=0, tiled=True),
        lax.all_gather(gain_mlp, ("row", "ctx"), axis=0, tiled=True),
        lax.all_gather(w_gate, ("row", "ctx"), axis=0, tiled=True),
        lax.all_gather(w_up, ("row", "ctx"), axis=0, tiled=True),
        lax.all_gather(w_down, ("row", "ctx"), axis=0, tiled=True),
    )
    resid = inputs + matmul(attn_tok, full_o)
    recip_mlp = lax.rsqrt(jnp.mean(resid * resid, axis=1, keepdims=True) + NORM_EPS)
    norm_mlp = resid * recip_mlp
    h_mlp = (norm_mlp * full_g2.astype(jnp.float32)[None, :]).astype(jnp.bfloat16)
    gate_pre = matmul(h_mlp, full_gate)
    up_pre = matmul(h_mlp, full_up)
    sigmoid = jax.nn.sigmoid(gate_pre)
    silu_gate = gate_pre * sigmoid
    hidden = (silu_gate * up_pre).astype(jnp.bfloat16)
    layer_out = (resid + matmul(hidden, full_down)).astype(jnp.bfloat16)[None]
    back_o, back_g2, back_gate, back_up, back_down = (
        lax.all_gather(w_output, ("row", "ctx"), axis=0, tiled=True),
        lax.all_gather(gain_mlp, ("row", "ctx"), axis=0, tiled=True),
        lax.all_gather(w_gate, ("row", "ctx"), axis=0, tiled=True),
        lax.all_gather(w_up, ("row", "ctx"), axis=0, tiled=True),
        lax.all_gather(w_down, ("row", "ctx"), axis=0, tiled=True),
    )
    grad_out = cotangent[0]
    grad_hidden = matmul_nt(grad_out, back_down)
    grad_gate_pre = (grad_hidden * up_pre * sigmoid * (1.0 + gate_pre * (1.0 - sigmoid))).astype(
        jnp.bfloat16
    )
    grad_up_pre = (grad_hidden * silu_gate).astype(jnp.bfloat16)
    grad_hmlp = matmul_nt(grad_gate_pre, back_gate) + matmul_nt(grad_up_pre, back_up)
    gain_mlp_term = jnp.sum(grad_hmlp * norm_mlp, axis=0)
    grad_norm_mlp = grad_hmlp * back_g2.astype(jnp.float32)[None, :]
    grad_resid = recip_mlp * (
        grad_norm_mlp - norm_mlp * jnp.mean(grad_norm_mlp * norm_mlp, axis=1, keepdims=True)
    ) + grad_out.astype(jnp.float32)
    grad_branch = grad_resid.astype(jnp.bfloat16)
    grad_attn_tok = matmul_nt(grad_branch, back_o).astype(jnp.bfloat16)
    grad_heads = lax.all_to_all(grad_attn_tok, "head", split_axis=1, concat_axis=0, tiled=True)
    grad_o = (
        grad_heads.reshape(block_rows, local_groups, group_size, HD).transpose(1, 2, 0, 3)
        * q_valid.astype(jnp.bfloat16)[None, None, :, None]
    )
    delta = jnp.sum(grad_o.astype(jnp.float32) * attn_heads, axis=3)

    def back_block(carry, block, key_start):
        grad_qacc, grad_keyval = carry
        scores = block_scores(block, key_start)
        probs_full = jnp.exp(scores - log_total[..., None])
        grad_vals = jnp.einsum(
            "gpqk,gpqd->kgd",
            probs_full.astype(jnp.bfloat16),
            grad_o,
            preferred_element_type=jnp.float32,
        )
        grad_probs = jnp.einsum(
            "gpqd,kgd->gpqk", grad_o, block[:, :, 1], preferred_element_type=jnp.float32
        )
        grad_scores = (probs_full * (grad_probs - delta[..., None])).astype(jnp.bfloat16)
        grad_qacc = (
            grad_qacc
            + jnp.einsum(
                "gpqk,kgd->gpqd", grad_scores, block[:, :, 0], preferred_element_type=jnp.float32
            )
            * score_scale
        )
        grad_keys = (
            jnp.einsum("gpqk,qgpd->kgd", grad_scores, q_blocks, preferred_element_type=jnp.float32)
            * score_scale
        )
        old_rows = lax.dynamic_slice_in_dim(grad_keyval, key_start, block_rows, 0)
        grad_keyval = lax.dynamic_update_slice_in_dim(
            grad_keyval, old_rows + jnp.stack([grad_keys, grad_vals], axis=2), key_start, 0
        )
        return (grad_qacc, grad_keyval)

    start_back = (
        jnp.zeros(stat_shape + (HD,), jnp.float32),
        jnp.zeros((n_ctx * block_rows, local_groups, 2, HD), jnp.float32),
    )
    grad_qacc, grad_keyval = over_blocks(
        back_block, start_back, lax.all_gather(head_kv, "ctx", axis=0, tiled=True), jnp.int32(0)
    )
    kv_summed = lax.psum_scatter(
        grad_keyval.reshape(n_ctx * block_rows, local_groups * 2 * HD).astype(jnp.bfloat16),
        "ctx",
        scatter_dimension=0,
        tiled=True,
    ).astype(jnp.float32)
    kv_summed = kv_summed.reshape(block_rows, local_groups, 2, HD)
    grad_key_pre = rotate(kv_summed[:, :, 0], q_cosine, -q_sine)
    packed_back = (
        jnp.stack([grad_key_pre, kv_summed[:, :, 1]], axis=2)
        .astype(jnp.bfloat16)
        .reshape(block_rows, local_groups * 2 * HD)
    )
    grad_q_rows = grad_qacc.transpose(2, 0, 1, 3).reshape(block_rows, local_heads, HD)
    grad_q_low = (
        rotate(grad_q_rows, q_cosine, -q_sine)
        .astype(jnp.bfloat16)
        .reshape(block_rows, local_heads * HD)
    )
    grad_q_tok, grad_kv_tok = (
        lax.all_to_all(grad_q_low, "head", split_axis=0, concat_axis=1, tiled=True),
        lax.all_to_all(packed_back, "head", split_axis=0, concat_axis=1, tiled=True),
    )
    grad_kv_tok = grad_kv_tok.reshape(tok_count, KV, 2, HD)
    grad_k_tok = grad_kv_tok[:, :, 0].reshape(tok_count, kv_width)
    grad_v_tok = grad_kv_tok[:, :, 1].reshape(tok_count, kv_width)
    piece_q = lax.all_gather(w_query, ("row", "ctx"), axis=0, tiled=True)
    piece_k = lax.all_gather(w_key, ("row", "ctx"), axis=0, tiled=True)
    piece_v = lax.all_gather(w_value, ("row", "ctx"), axis=0, tiled=True)
    piece_g = lax.all_gather(gain_attn, ("row", "ctx"), axis=0, tiled=True)
    partial_grad = (
        matmul_nt(grad_q_tok, piece_q)
        + matmul_nt(grad_k_tok, piece_k)
        + matmul_nt(grad_v_tok, piece_v)
    )
    grad_hattn = partial_grad
    grad_nattn = partial_grad * piece_g.astype(jnp.float32)[None, :]
    grad_hattn, grad_nattn = (grad_hattn, grad_nattn)
    gain_attn_term = jnp.sum(grad_hattn * norm_attn, axis=0)
    grad_inputs = grad_resid + recip_attn * (
        grad_nattn - norm_attn * jnp.mean(grad_nattn * norm_attn, axis=1, keepdims=True)
    )
    tokens_grad = grad_inputs.astype(jnp.bfloat16)[None]
    gains_local = jnp.stack([gain_attn_term, gain_mlp_term], axis=1)
    summed_down = lax.psum_scatter(
        matmul_tn(hidden, grad_out).astype(jnp.bfloat16),
        ("row", "ctx"),
        scatter_dimension=0,
        tiled=True,
    ).astype(jnp.float32)
    gain_block = jnp.pad(gains_local, ((0, 0), (0, 126)))
    summed = lax.psum_scatter(
        jnp.concatenate(
            [
                matmul_tn(attn_tok, grad_branch),
                matmul_tn(h_attn, grad_q_tok),
                matmul_tn(h_attn, grad_k_tok),
                matmul_tn(h_attn, grad_v_tok),
                matmul_tn(h_mlp, grad_gate_pre),
                matmul_tn(h_mlp, grad_up_pre),
                gain_block,
            ],
            axis=1,
        ).astype(jnp.bfloat16),
        ("row", "ctx"),
        scatter_dimension=0,
        tiled=True,
    ).astype(jnp.float32)
    summed, summed_down = (
        lax.psum(summed.astype(jnp.bfloat16), "head").astype(jnp.float32),
        lax.psum(summed_down.astype(jnp.bfloat16), "head").astype(jnp.float32),
    )
    edge_b = model_width + model_width
    edge_c = edge_b + kv_width
    edge_d = edge_c + kv_width
    edge_e = edge_d + hidden_width
    edge_f = edge_e + hidden_width
    return (
        layer_out,
        tokens_grad,
        summed[:, model_width:edge_b],
        summed[:, edge_b:edge_c],
        summed[:, edge_c:edge_d],
        summed[:, 0:model_width],
        summed[:, edge_d:edge_e],
        summed[:, edge_e:edge_f],
        summed_down,
        summed[:, edge_f],
        summed[:, edge_f + 1],
    )


def solution(mesh):
    return jax.shard_map(
        body,
        mesh=mesh,
        in_specs=(
            P("row", ("ctx", "head"), None),
            P("row", None),
            P(("row", "ctx"), None),
            P(("row", "ctx"), None),
            P(("row", "ctx"), None),
            P(("row", "ctx"), None),
            P(("row", "ctx"), None),
            P(("row", "ctx"), None),
            P(("row", "ctx"), None),
            P(("row", "ctx")),
            P(("row", "ctx")),
            P("row", ("ctx", "head"), None),
        ),
        out_specs=(
            P("row", ("ctx", "head"), None),
            P("row", ("ctx", "head"), None),
            P(("row", "ctx"), None),
            P(("row", "ctx"), None),
            P(("row", "ctx"), None),
            P(("row", "ctx"), None),
            P(("row", "ctx"), None),
            P(("row", "ctx"), None),
            P(("row", "ctx"), None),
            P(("row", "ctx")),
            P(("row", "ctx")),
        ),
        check_vma=False,
    )
```

profile of v0, /device:TPU:27, one launch (start us, length us, event | category | flops | bytes accessed | tf_op | source)
XLA Modules:
  0.0 1260.2 jit_solution(298635216196908631)
XLA Ops:
  13.1 25.1 %all-reduce.4 = (bf16[1536]{0:T(1024)(128)(2,1)S(1)}, bf16[1536]{0:T(1024)(128)(2,1)S(1)}) all-reduce(bf16[1536]{0:T(1024)(128)(2,1)S(1)} %dynamic-update-slice, bf16[1536]{0:T(1024)(128)(2,1)S(1)} %dynamic-update-slice.1), channel_id=1, replica_groups=mesh['row'=4,'ctx'=4,'head'=8] {'row','ctx'}, use_global_device_ids=true, to_apply=%add.2 | all-reduce | flops 3072 | bytes 12288
  49.6 33.6 %all-gather.9.cloned.1.call-done = bf16[1536,768]{1,0:T(8,128)(2,1)} async-done(((bf16[96,768]{1,0:T(8,128)(2,1)}), bf16[1536,768]{1,0:T(8,128)(2,1)}) %all-gather.9.cloned.1.call-update) | async-done | bytes 2359312 | tf_op jit(solution)/shard_map/all_gather | solution.py:112
  90.9 12.9 %all_to_all.93 = bf16[128,8,192]{0,2,1:T(8,128)(2,1)S(1)} all-to-all(bf16[128,8,192]{0,2,1:T(8,128)(2,1)S(1)} %bitcast.792), channel_id=1, replica_groups=mesh['row'=4,'ctx'=4,'head'=8] {'head'}, dimensions={1} | all-to-all | bytes 786432 | tf_op jit(solution)/shard_map/all_to_all | solution.py:131
  107.4 19.1 %all-gather.15.cloned.1.call-done = bf16[1536,1536]{1,0:T(8,128)(2,1)} async-done(((bf16[96,1536]{1,0:T(8,128)(2,1)}), bf16[1536,1536]{1,0:T(8,128)(2,1)}) %all-gather.15.cloned.1.call-update) | async-done | bytes 4718608 | tf_op jit(solution)/shard_map/all_gather | solution.py:111
  137.8 7.3 all-to-all-start.1
  145.1 12.6 all-gather.13.cloned.1.call-done
  160.3 9.4 conditional.8
  169.8 8.4 conditional.9
  178.3 8.2 conditional.10
  186.4 8.2 conditional.11
  195.6 15.1 %all-to-all-start.2 = ((bf16[8,128,192]{1,2,0:T(8,128)(2,1)}), bf16[8,128,192]{1,2,0:T(8,128)(2,1)S(1)}, u32[]{:S(2)}, u32[]{:S(2)}) async-start(bf16[8,128,192]{1,2,0:T(8,128)(2,1)} %copy.221), calls=%async_computation.2 | async-start | bytes 786432 | tf_op jit(solution)/shard_map/all_to_all | solution.py:199
  214.4 61.9 %all-gather.19.cloned.1.call-done = bf16[1536,4096]{1,0:T(8,128)(2,1)} async-done(((bf16[96,4096]{1,0:T(8,128)(2,1)}), bf16[1536,4096]{1,0:T(8,128)(2,1)}) %all-gather.19.cloned.1.call-update) | async-done | bytes 12582928 | tf_op jit(solution)/shard_map/all_gather | solution.py:203
  276.3 7.8 fusion.273
  284.1 66.9 %all-gather.21.cloned.1.call-done = bf16[1536,4096]{1,0:T(8,128)(2,1)} async-done(((bf16[96,4096]{1,0:T(8,128)(2,1)}), bf16[1536,4096]{1,0:T(8,128)(2,1)}) %all-gather.21.cloned.1.call-update) | async-done | bytes 12582928 | tf_op jit(solution)/shard_map/all_gather | solution.py:204
  350.9 7.8 fusion.274
  358.7 66.8 %all-gather.23.cloned.1.call-done = bf16[4096,1536]{1,0:T(8,128)(2,1)} async-done(((bf16[256,1536]{1,0:T(8,128)(2,1)}), bf16[4096,1536]{1,0:T(8,128)(2,1)}) %all-gather.23.cloned.1.call-update) | async-done | bytes 12582928 | tf_op jit(solution)/shard_map/all_gather | solution.py:205
  425.6 11.8 multiply_convert_fusion
  437.3 10.2 fusion.275
  447.6 7.1 multiply_reduce_fusion
  477.9 19.8 %conditional.12 = (f32[1,2,1024,96]{2,3,1,0:T(8,128)S(1)}, f32[4096,1,2,96]{0,3,2,1:T(8,128)}) conditional(s32[]{:T(128)} %convert_element_type.245, () %tuple.65, (s32[1024]{0:T(1024)S(1)}, s32[8]{0:T(128)S(1)}, s32[1024]{0:T(1024)S(1)}, bf16[1024,1,2,96]{0,3,2,1:T(8,128)(2,1)}, bf16[1024,1,2,96]{0,3,2,1:T(8,128)(2,1)S(1)}, ...), branch_computations={%region_32.33_spmd, %region_33.36_spmd} | conditional | flops 2040847360 | bytes 76914912 | solution.py:176
  497.7 18.6 %conditional.13 = ((f32[1,2,1024,96]{2,3,1,0:T(8,128)S(1)}, f32[4096,1,2,96]{0,3,2,1:T(8,128)})) conditional(s32[]{:T(128)} %convert_element_type.244, (f32[1,2,1024,96]{2,3,1,0:T(8,128)S(1)}, f32[4096,1,2,96]{0,3,2,1:T(8,128)}) %conditional.12, (s32[1024]{0:T(1024)S(1)}, s32[8]{0:T(128)S(1)}, s32[1024]{0:T(1024)S(1)}, ...), branch_computations={%region_36.37_spmd, %region_37.40_spmd} | conditional | flops 2038292480 | bytes 74567880 | solution.py:176
  516.3 19.4 %conditional.14 = ((f32[1,2,1024,96]{2,3,1,0:T(8,128)S(1)}, f32[4096,1,2,96]{0,3,2,1:T(8,128)})) conditional(s32[]{:T(128)} %convert_element_type.243, (f32[1,2,1024,96]{2,3,1,0:T(8,128)S(1)}, f32[4096,1,2,96]{0,3,2,1:T(8,128)}) %get-tuple-element.414, (s32[1024]{0:T(1024)S(1)}, s32[8]{0:T(128)S(1)}, s32[1024]{0:T(1024)S(1)}, ...), branch_computations={%region_40.41_spmd, %region_41.44_spmd} | conditional | flops 2038292480 | bytes 76140776 | solution.py:176
  535.7 19.6 %conditional.15 = ((f32[1,2,1024,96]{2,3,1,0:T(8,128)S(1)}, f32[4096,1,2,96]{0,3,2,1:T(8,128)})) conditional(s32[]{:T(128)} %convert_element_type.242, (f32[1,2,1024,96]{2,3,1,0:T(8,128)S(1)}, f32[4096,1,2,96]{0,3,2,1:T(8,128)}) %get-tuple-element.415, (s32[1024]{0:T(1024)S(1)}, s32[8]{0:T(128)S(1)}, s32[1024]{0:T(1024)S(1)}, ...), branch_computations={%region_44.45_spmd, %region_45.48_spmd} | conditional | flops 2038292480 | bytes 76140776 | solution.py:176
  558.8 9.4 convolution_convert_fusion
  575.6 6.7 copy.227
  584.3 7.6 all-to-all-start.4
  614.9 7.4 all-to-all-start.5
  655.5 7.9 fusion.210
  671.0 58.2 %reduce-scatter.8.cloned.1.call-done = bf16[256,1536]{1,0:T(8,128)(2,1)} async-done(((bf16[4096,1536]{1,0:T(8,128)(2,1)}), bf16[256,1536]{1,0:T(8,128)(2,1)}) %reduce-scatter.8.cloned.1.call-update) | async-done | bytes 786448 | tf_op jit(solution)/shard_map/reduce_scatter | solution.py:327
  729.1 416.7 %reduce-scatter.6.cloned.1.call-done = bf16[96,12928]{1,0:T(8,128)(2,1)} async-done(((bf16[1536,12928]{1,0:T(8,128)(2,1)}), bf16[96,12928]{1,0:T(8,128)(2,1)}) %reduce-scatter.6.cloned.1.call-update) | async-done | bytes 2482192 | tf_op jit(solution)/shard_map/reduce_scatter | solution.py:334
  1145.9 7.5 fusion.212
  1154.4 88.6 %all-reduce.8.cloned.1.call-done = (bf16[96,12928]{1,0:T(8,128)(2,1)}, bf16[256,1536]{1,0:T(8,128)(2,1)}) async-done(((bf16[96,12928]{1,0:T(8,128)(2,1)}, bf16[256,1536]{1,0:T(8,128)(2,1)}), (bf16[96,12928]{1,0:T(8,128)(2,1)}, bf16[256,1536]{1,0:T(8,128)(2,1)})) %all-reduce.8.cloned.1.call-update) | async-done | bytes 3268624 | tf_op jit(solution)/shard_map/psum | solution.py:352
  (286 shorter events, 267.5 us)
Async XLA Ops:
  7.2 80.3 %copy-start.1 = (bf16[1,128,1536]{2,1,0:T(8,128)(2,1)S(1)}, bf16[1,128,1536]{2,1,0:T(8,128)(2,1)}, u32[]{:S(2)}) copy-start(bf16[1,128,1536]{2,1,0:T(8,128)(2,1)} %param.30) | copy-start | bytes 1179652
  7.2 39.6 %all-gather.11.cloned.1.call-start = ((), (), s32[]{:S(2)}) async-start(), calls=%async_computation.10 | async-start | bytes 2506752 | tf_op jit(solution)/shard_map/all_gather | solution.py:113
  7.9 75.2 %all-gather.9.cloned.1.call-start = ((), (), s32[]{:S(2)}) async-start(), calls=%async_computation.9 | async-start | bytes 2506752 | tf_op jit(solution)/shard_map/all_gather | solution.py:112
  8.7 117.8 %all-gather.15.cloned.1.call-start = ((), (), s32[]{:S(2)}) async-start(), calls=%async_computation.12 | async-start | bytes 5013504 | tf_op jit(solution)/shard_map/all_gather | solution.py:111
  9.4 148.3 %all-gather.13.cloned.1.call-start = ((), (), s32[]{:S(2)}) async-start(), calls=%async_computation.11 | async-start | bytes 1966080 | tf_op jit(solution)/shard_map/all_gather | solution.py:191
  38.2 94.9 %copy-start.20 = (f32[1536]{0:T(1024)}, f32[1536]{0:T(1024)S(1)}, u32[]{:S(2)}) copy-start(f32[1536]{0:T(1024)S(1)} %convert_element_type.248) | copy-start | bytes 18436
  42.2 90.9 %copy-start.27 = (f32[128]{0:T(128)}, f32[128]{0:T(128)S(1)}, u32[]{:S(2)}) copy-start(f32[128]{0:T(128)S(1)} %add_rsqrt_fusion.1) | copy-start | bytes 1540
  104.6 106.2 %all-gather.17.cloned.1.call-start = ((), (), s32[]{:S(2)}) async-start(), calls=%async_computation.13 | async-start | bytes 5013504 | tf_op jit(solution)/shard_map/all_gather | solution.py:201
  105.2 171.1 %all-gather.19.cloned.1.call-start = ((), (), s32[]{:S(2)}) async-start(), calls=%async_computation.14 | async-start | bytes 13369344 | tf_op jit(solution)/shard_map/all_gather | solution.py:203
  105.8 245.1 %all-gather.21.cloned.1.call-start = ((), (), s32[]{:S(2)}) async-start(), calls=%async_computation.15 | async-start | bytes 13369344 | tf_op jit(solution)/shard_map/all_gather | solution.py:204
  106.6 319.0 %all-gather.23.cloned.1.call-start = ((), (), s32[]{:S(2)}) async-start(), calls=%async_computation.16 | async-start | bytes 13369344 | tf_op jit(solution)/shard_map/all_gather | solution.py:205
  133.1 27.2 %copy-start.32 = (s32[1,8]{1,0:T(1,128)S(1)}, s32[1,8]{1,0:T(1,128)}, u32[]{:S(2)}) copy-start(s32[1,8]{1,0:T(1,128)} %param.31) | copy-start | bytes 100
  137.8 22.1 %all-to-all-start.1 = ((bf16[128,8,192]{0,2,1:T(8,128)(2,1)}), bf16[128,8,192]{0,2,1:T(8,128)(2,1)S(1)}, u32[]{:S(2)}, u32[]{:S(2)}) async-start(bf16[128,8,192]{0,2,1:T(8,128)(2,1)} %bitcast.184), calls=%async_computation.1 | async-start | bytes 786432 | tf_op jit(solution)/shard_map/all_to_all | solution.py:130
  159.9 18.4 %copy-start.15 = (bf16[1024,192]{0,1:T(8,128)(2,1)}, bf16[1024,192]{0,1:T(8,128)(2,1)S(1)}, u32[]{:S(2)}) copy-start(bf16[1024,192]{0,1:T(8,128)(2,1)S(1)} %get-tuple-element.345) | copy-start | bytes 1179652
  159.9 26.6 %copy-start.13 = (bf16[1024,192]{0,1:T(8,128)(2,1)}, bf16[1024,192]{0,1:T(8,128)(2,1)S(1)}, u32[]{:S(2)}) copy-start(bf16[1024,192]{0,1:T(8,128)(2,1)S(1)} %get-tuple-element.344) | copy-start | bytes 1179652
  194.6 89.5 %copy-start.5 = (f32[1,2,1024,96]{2,3,1,0:T(8,128)}, f32[1,2,1024,96]{2,3,1,0:T(8,128)S(1)}, u32[]{:S(2)}) copy-start(f32[1,2,1024,96]{2,3,1,0:T(8,128)S(1)} %get-tuple-element.271) | copy-start | bytes 2359300
  195.6 15.2 %all-to-all-start.2 = ((bf16[8,128,192]{1,2,0:T(8,128)(2,1)}), bf16[8,128,192]{1,2,0:T(8,128)(2,1)S(1)}, u32[]{:S(2)}, u32[]{:S(2)}) async-start(bf16[8,128,192]{1,2,0:T(8,128)(2,1)} %copy.221), calls=%async_computation.2 | async-start | bytes 786432 | tf_op jit(solution)/shard_map/all_to_all | solution.py:199
  210.8 73.3 %copy-start.7 = (bf16[8,128,192]{1,2,0:T(8,128)(2,1)}, bf16[8,128,192]{1,2,0:T(8,128)(2,1)S(1)}, u32[]{:S(2)}) copy-start(bf16[8,128,192]{1,2,0:T(8,128)(2,1)S(1)} %all-to-all-done.2) | copy-start | bytes 1179652
  350.9 74.6 %copy-start.12 = (bf16[1,128,1536]{2,1,0:T(8,128)(2,1)S(1)}, bf16[1,128,1536]{2,1,0:T(8,128)(2,1)}, u32[]{:S(2)}) copy-start(bf16[1,128,1536]{2,1,0:T(8,128)(2,1)} %param.41) | copy-start | bytes 1179652
  437.3 10.2 copy-start
  454.6 22.3 %copy-start.6 = (f32[1,2,1024,96]{2,3,1,0:T(8,128)S(1)}, f32[1,2,1024,96]{2,3,1,0:T(8,128)}, u32[]{:S(2)}) copy-start(f32[1,2,1024,96]{2,3,1,0:T(8,128)} %copy-done.5) | copy-start | bytes 2359300
  462.0 12.8 %all-to-all-start.3 = ((bf16[128,8,192]{0,2,1:T(8,128)(2,1)}), bf16[128,8,192]{0,2,1:T(8,128)(2,1)S(1)}, u32[]{:S(2)}, u32[]{:S(2)}) async-start(bf16[128,8,192]{0,2,1:T(8,128)(2,1)} %bitcast.789), calls=%async_computation.3 | async-start | bytes 786432 | tf_op jit(solution)/shard_map/all_to_all | solution.py:238
  468.6 143.4 %reduce-scatter.4.cloned.1.call-start = ((), (), s32[]{:S(2)}) async-start(), calls=%async_computation.17 | async-start | bytes 1966080 | tf_op jit(solution)/shard_map/reduce_scatter | solution.py:283
  477.9 19.8 %copy-start.18 = (bf16[1024,192]{0,1:T(8,128)(2,1)S(1)}, bf16[1024,192]{0,1:T(8,128)(2,1)}, u32[]{:S(2)}) copy-start(bf16[1024,192]{0,1:T(8,128)(2,1)} %copy-done.17) | copy-start | bytes 1179652
  558.5 170.6 %reduce-scatter.8.cloned.1.call-start = ((), (), s32[]{:S(2)}) async-start(), calls=%async_computation.19 | async-start | bytes 13369344 | tf_op jit(solution)/shard_map/reduce_scatter | solution.py:327
  582.3 14.6 %copy-start.21 = (f32[1536]{0:T(1024)S(1)}, f32[1536]{0:T(1024)}, u32[]{:S(2)}) copy-start(f32[1536]{0:T(1024)} %copy-done.20) | copy-start | bytes 18436
  582.3 14.6 %copy-start.28 = (f32[128]{0:T(128)S(1)}, f32[128]{0:T(128)}, u32[]{:S(2)}) copy-start(f32[128]{0:T(128)} %copy-done.27) | copy-start | bytes 1540
  584.3 12.6 all-to-all-start.4
  614.9 12.6 %all-to-all-start.5 = ((bf16[8,128,192]{1,2,0:T(8,128)(2,1)}), bf16[8,128,192]{1,2,0:T(8,128)(2,1)}, u32[]{:S(2)}, u32[]{:S(2)}) async-start(bf16[8,128,192]{1,2,0:T(8,128)(2,1)} %copy.225), calls=%async_computation.6 | async-start | bytes 786432 | tf_op jit(solution)/shard_map/all_to_all | solution.py:304
  622.2 523.6 %reduce-scatter.6.cloned.1.call-start = ((), (), s32[]{:S(2)}) async-start(), calls=%async_computation.18 | async-start | bytes 42196992 | tf_op jit(solution)/shard_map/reduce_scatter | solution.py:334
  627.5 15.0 %copy-start.9 = (f32[128,1536]{1,0:T(8,128)S(1)}, f32[128,1536]{1,0:T(8,128)}, u32[]{:S(2)}) copy-start(f32[128,1536]{1,0:T(8,128)} %fusion.276) | copy-start | bytes 2359300
  670.9 572.0 %all-reduce.8.cloned.1.call-start = ((), (), s32[]{:S(2)}) async-start(), calls=%async_computation.20 | async-start | bytes 6537216 | tf_op jit(solution)/shard_map/psum | solution.py:352
  (26 other events, 149.3 us)
Sparse Core Ops, SparseCore 0:
  9.7 36.9 all-gather.10
  48.4 34.6 all-gather.8
  84.9 41.5 all-gather.14
  128.6 29.0 all-gather.12
  159.2 42.5 all-gather.16
  203.4 72.8 all-gather.18
  278.0 72.8 all-gather.20
  352.6 72.8 all-gather.22
  558.7 23.6 reduce-scatter.3
  584.7 144.4 reduce-scatter.7
  731.6 414.2 reduce-scatter.5
  1148.3 94.5 all-reduce.7
where the time goes:
time: 1280 us; the launch traced here: 1260 us
  waiting for transfers between devices  838 us (65%)
  matrix products  196 us (15%)
  local copies, waits for them, and re-layouts  79 us (6%)
  other arithmetic  46.7 us (4%)
  starting transfers between devices  44.9 us (4%)
  blocking collectives  38 us (3%)
  between operations  15.9 us (1%)
    reduce_scatter x1, waiting for transfers between devices, body(): lax.psum_scatter(jnp.concatenate([matmul_tn(attn_tok, grad_branch), matmu...  417 us
    psum x1, waiting for transfers between devices, body(): lax.psum(summed.astype(jnp.bfloat16), 'head').astype(jnp.float32)  88.6 us
    all_gather x1, waiting for transfers between devices, body(): lax.all_gather(w_up, ('row', 'ctx'), axis=0, tiled=True)  66.9 us
    all_gather x1, waiting for transfers between devices, body(): lax.all_gather(w_down, ('row', 'ctx'), axis=0, tiled=True)  66.8 us
    all_gather x1, waiting for transfers between devices, body(): lax.all_gather(w_gate, ('row', 'ctx'), axis=0, tiled=True)  61.9 us
    reduce_scatter x1, waiting for transfers between devices, body(): lax.psum_scatter(matmul_tn(hidden, grad_out).astype(jnp.bfloat16), ('row'...  58.2 us
    dot_general x7, matrix products, matmul_nt(): lax.dot_general(left_side, right_side, (((1,), (1,)), ((), ())), preferre...  43.5 us
    dot_general x7, matrix products, matmul_tn(): lax.dot_general(left_side, right_side, (((0,), (0,)), ((), ())), preferre...  36.6 us
  transfers between devices with their start and end apart: 17, of which 12 were waited for; matrix products, arithmetic and copies ran while one was open for 15% of the time, Pallas kernels for 0%

commit v1 on v0

v1 whole, which is shorter than its diff:
```python
from functools import partial

import jax
import jax.numpy as jnp
import numpy as np
from jax import lax
from jax.experimental import pallas as pl
from jax.experimental.pallas import tpu as pltpu
from jax.sharding import Mesh
from jax.sharding import PartitionSpec as P

HEADS = 16
KV = 8
HD = 96
NORM_EPS = 1e-05
LOG2E = 1.4426950408889634
LN2 = 0.6931471805599453
SCALE = HD ** (-0.5)
BF = jnp.bfloat16
F32 = jnp.float32
AXES = ("z", "yl", "c", "yh", "x")
GROUP = ("yl", "c", "yh")
MESH = pl.DeviceIdType.MESH
TOK = 128
NT = 8
NX = 4


def frequency_table(head_width):
    halfway = head_width // 2
    base_freq = 500000.0 ** (-np.arange(halfway) * 2.0 / head_width)
    wavelength = 2.0 * np.pi / base_freq
    smooth = (8192.0 / wavelength - 1.0) / 3.0
    middle = (1.0 - smooth) * base_freq / 32.0 + smooth * base_freq
    freq_table = np.where(
        wavelength > 8192.0, base_freq / 32.0, np.where(wavelength < 2048.0, base_freq, middle)
    )
    return freq_table.astype(np.float32)


def doc_layout(lengths, places):
    doc_count = lengths.shape[0]
    doc_ends = jnp.cumsum(lengths)
    starts = doc_ends - lengths
    segment = jnp.sum((places[:, None] >= doc_ends[None, :]).astype(jnp.int32), axis=1)
    chosen = segment[:, None] == jnp.arange(doc_count, dtype=jnp.int32)[None, :]
    offset = jnp.sum(jnp.where(chosen, starts[None, :], 0), axis=1) + jnp.where(
        segment == doc_count, doc_ends[doc_count - 1], 0
    )
    return (segment, offset)


def mm(a, b):
    return jnp.dot(a, b, preferred_element_type=F32)


def mm_nt(a, b):
    return lax.dot_general(a, b, (((1,), (1,)), ((), ())), preferred_element_type=F32)


def mm_tn(a, b):
    return lax.dot_general(a, b, (((0,), (0,)), ((), ())), preferred_element_type=F32)


class Place:
    def __init__(self):
        self.yl = lax.axis_index("yl")
        self.c = lax.axis_index("c")
        self.yh = lax.axis_index("yh")
        self.y = self.yh * 2 + self.yl
        self.t = self.rank(0, self.c)

    def rank(self, k, c):
        y = lax.rem(self.y + (k + 4), 4)
        return lax.rem(y, 2) * 4 + c * 2 + y // 2

    def ring(self, k):
        y = lax.rem(self.y + (k + 4), 4)
        return {"yh": y // 2, "yl": lax.rem(y, 2)}

    def sibling(self):
        return {"c": 1 - self.c}

    def greet(self):
        barrier = pltpu.get_barrier_semaphore()
        for who in (self.ring(1), self.ring(-1), self.sibling()):
            pl.semaphore_signal(barrier, inc=1, device_id=who, device_id_type=MESH)
        pl.semaphore_wait(barrier, 3)


class Sent:
    def __init__(self, copy):
        self.copy, self.arrived = copy, False

    def wait_recv(self):
        if not self.arrived:
            self.copy.wait_recv()
        self.arrived = True

    def wait_send(self):
        self.copy.wait_send()


class Copies:
    def __init__(self, send_sem, recv_sem):
        self.send_sem, self.recv_sem, self.n, self.all = send_sem, recv_sem, 0, []

    def __call__(self, src, dst, who):
        i = self.n
        self.n += 1
        copy = pltpu.make_async_remote_copy(
            src_ref=src,
            dst_ref=dst,
            send_sem=self.send_sem.at[i],
            recv_sem=self.recv_sem.at[i],
            device_id=who,
            device_id_type=MESH,
        )
        copy.start()
        sent = Sent(copy)
        self.all.append(sent)
        return sent

    def finish(self):
        for sent in self.all:
            sent.wait_recv()
        for sent in self.all:
            sent.wait_send()


def gather_begin(me, send, own, out):
    return [
        send(own, out.at[me.t], me.ring(1)),
        send(own, out.at[me.t], me.ring(-1)),
        send(own, out.at[me.t], me.sibling()),
    ]


def gather_rest(me, send, out, begun):
    down, up, mine = begun
    half = out.shape[1] // 2
    below, above, far = me.rank(-1, me.c), me.rank(1, me.c), me.rank(2, me.c)
    down.wait_recv()
    part = out.at[below, pl.ds(0, half)]
    on_down = send(part, part, me.ring(1))
    sib_below = send(out.at[below], out.at[below], me.sibling())
    up.wait_recv()
    part = out.at[above, pl.ds(half, half)]
    on_up = send(part, part, me.ring(-1))
    sib_above = send(out.at[above], out.at[above], me.sibling())
    on_down.wait_recv()
    on_up.wait_recv()
    sib_far = send(out.at[far], out.at[far], me.sibling())
    for copy in (mine, sib_below, sib_above, sib_far):
        copy.wait_recv()


def gather_kernel(own, out, send_sem, recv_sem, local_sem):
    me = Place()
    me.greet()
    send = Copies(send_sem, recv_sem)
    begun = gather_begin(me, send, own, out)
    local = pltpu.make_async_copy(own, out.at[me.t], local_sem)
    local.start()
    gather_rest(me, send, out, begun)
    local.wait()
    send.finish()


ANY = pl.BlockSpec(memory_space=pl.ANY)


def gather_group(own, name, number):
    rows, width = own.shape
    return pl.pallas_call(
        gather_kernel,
        out_shape=jax.ShapeDtypeStruct((NT, rows, width), own.dtype),
        in_specs=[ANY],
        out_specs=ANY,
        scratch_shapes=[
            pltpu.SemaphoreType.DMA((8,)),
            pltpu.SemaphoreType.DMA((8,)),
            pltpu.SemaphoreType.DMA,
        ],
        compiler_params=pltpu.CompilerParams(collective_id=number, has_side_effects=True),
        name=name,
    )(own)


def scatter_kernel(part, out, sib, far_a, far_b, near_a, near_b, mid, send_sem, recv_sem):
    me = Place()
    me.greet()
    send = Copies(send_sem, recv_sem)
    half = TOK // 2
    lo, hi = pl.ds(0, half), pl.ds(half, half)
    other = 1 - me.c
    from_sib = {}
    for k in (2, 1, 3, 0):
        from_sib[k] = send(part.at[me.rank(k, other)], sib.at[k], me.sibling())

    def both(k, rows):
        return part[me.rank(k, me.c), rows].astype(F32) + sib[k, rows].astype(F32)

    from_sib[2].wait_recv()
    mid[2] = both(2, slice(None)).astype(BF)
    far_up = send(mid.at[2, lo], far_a, me.ring(1))
    far_down = send(mid.at[2, hi], far_b, me.ring(-1))
    from_sib[1].wait_recv()
    mid[1, half:] = both(1, slice(half, TOK)).astype(BF)
    up_hi = send(mid.at[1, hi], near_a.at[hi], me.ring(1))
    from_sib[3].wait_recv()
    mid[3, :half] = both(3, slice(0, half)).astype(BF)
    down_lo = send(mid.at[3, lo], near_b.at[lo], me.ring(-1))
    far_up.wait_recv()
    mid[1, :half] = (both(1, slice(0, half)) + far_a[...].astype(F32)).astype(BF)
    up_lo = send(mid.at[1, lo], near_a.at[lo], me.ring(1))
    far_down.wait_recv()
    mid[3, half:] = (both(3, slice(half, TOK)) + far_b[...].astype(F32)).astype(BF)
    down_hi = send(mid.at[3, hi], near_b.at[hi], me.ring(-1))
    from_sib[0].wait_recv()
    total = both(0, slice(None))
    for copy in (up_hi, up_lo, down_lo, down_hi):
        copy.wait_recv()
    out[...] = total + near_a[...].astype(F32) + near_b[...].astype(F32)
    send.finish()


VM = pl.BlockSpec(memory_space=pltpu.VMEM)


def scatter_group(part, name, number):
    _, rows, width = part.shape
    half = rows // 2
    return pl.pallas_call(
        scatter_kernel,
        out_shape=jax.ShapeDtypeStruct((rows, width), F32),
        in_specs=[VM],
        out_specs=VM,
        scratch_shapes=[
            pltpu.VMEM((4, rows, width), BF),
            pltpu.VMEM((half, width), BF),
            pltpu.VMEM((half, width), BF),
            pltpu.VMEM((rows, width), BF),
            pltpu.VMEM((rows, width), BF),
            pltpu.VMEM((4, rows, width), BF),
            pltpu.SemaphoreType.DMA((10,)),
            pltpu.SemaphoreType.DMA((10,)),
        ],
        compiler_params=pltpu.CompilerParams(
            collective_id=number, has_side_effects=True, vmem_limit_bytes=40 * 2**20
        ),
        name=name,
    )(part)


def first_kernel(
    tok, wqkv, wgu, wo, tok_all, qkv, gu, oh, tmp_qkv, tmp_gu, send_sem, recv_sem, local_sem
):
    me = Place()
    me.greet()
    send = Copies(send_sem, recv_sem)
    c, other = me.c, 1 - me.c
    step = 1 - 2 * c
    slot, slot_other = me.yl * 2 + c, me.yl * 2 + other
    toward, away = me.ring(step), me.ring(-step)
    t_toward, t_relay, t_sib = me.rank(step, c), me.rank(step, other), me.rank(0, other)
    pairs = ((wqkv, qkv, tmp_qkv), (wgu, gu, tmp_gu))
    kept = []

    def keep(src, dst):
        copy = pltpu.make_async_copy(src, dst, local_sem.at[len(kept)])
        copy.start()
        kept.append(copy)

    relays = [send(src.at[t_relay], tmp, me.sibling()) for src, _, tmp in pairs]
    for src, dst, _ in pairs:
        send(src.at[t_sib], dst.at[slot], me.sibling())
        send(src.at[t_toward], dst.at[slot], toward)
    send(wo, oh.at[me.yl], toward)
    begun = gather_begin(me, send, tok, tok_all)
    keep(tok, tok_all.at[me.t])
    keep(wo, oh.at[me.yl])
    for src, dst, _ in pairs:
        keep(src.at[me.t], dst.at[slot])
    for relay, (_, dst, tmp) in zip(relays, pairs):
        relay.wait_recv()
        send(tmp, dst.at[slot_other], away)
    gather_rest(me, send, tok_all, begun)
    for copy in kept:
        copy.wait()
    send.finish()


def first_gather(tok, wqkv, wgu, wo):
    def like(shape):
        return jax.ShapeDtypeStruct(shape, BF)

    rows = wo.shape[0]
    return pl.pallas_call(
        first_kernel,
        out_shape=(
            like((NT,) + tok.shape),
            like((4,) + wqkv.shape[1:]),
            like((4,) + wgu.shape[1:]),
            like((2,) + wo.shape),
            like(wqkv.shape[1:]),
            like(wgu.shape[1:]),
        ),
        in_specs=[ANY] * 4,
        out_specs=(ANY,) * 6,
        scratch_shapes=[
            pltpu.SemaphoreType.DMA((20,)),
            pltpu.SemaphoreType.DMA((20,)),
            pltpu.SemaphoreType.DMA((4,)),
        ],
        compiler_params=pltpu.CompilerParams(collective_id=0, has_side_effects=True),
        name="first_gather",
    )(tok, wqkv, wgu, wo)[:4]


QROWS = 2 * TOK
CHUNK = NX * TOK


def keys_of(ref, kt):
    return jnp.concatenate([ref[x, kt] for x in range(NX)], axis=0)


def attend_kernel(x_ref, q_ref, k_ref, v_ref, start_ref, o_ref, lse_ref):
    x = x_ref[0]

    def tile(t, kt, q, start, carry, diagonal):
        top, total, acc = carry
        s = mm_nt(q, keys_of(k_ref, kt))
        place = kt * CHUNK + lax.broadcasted_iota(jnp.int32, (QROWS, CHUNK), 1)
        keep = place >= start
        if diagonal:
            row = lax.broadcasted_iota(jnp.int32, (QROWS, CHUNK), 0)
            query = t * CHUNK + x * TOK + lax.rem(row, TOK)
            keep = keep & (place <= query)
        s = jnp.where(keep, s, -jnp.inf)
        new_top = jnp.maximum(top, jnp.max(s, axis=1, keepdims=True))
        p = jnp.exp2(s - new_top)
        factor = jnp.exp2(top - new_top)
        total = total * factor + jnp.sum(p, axis=1, keepdims=True)
        acc = acc * factor + mm(p.astype(BF), keys_of(v_ref, kt))
        return new_top, total, acc

    def one(t, _):
        q = jnp.concatenate([q_ref[0, t], q_ref[1, t]], axis=0)
        start = jnp.concatenate([start_ref[t]] * 2, axis=0)
        carry = (
            jnp.full((QROWS, 1), -1e30, F32),
            jnp.zeros((QROWS, 1), F32),
            jnp.zeros((QROWS, HD), F32),
        )
        carry = lax.fori_loop(0, t, lambda kt, c: tile(t, kt, q, start, c, False), carry)
        top, total, acc = tile(t, t, q, start, carry, True)
        o = acc / total
        lse = top + jnp.log2(total)
        o_ref[0, t], o_ref[1, t] = o[:TOK], o[TOK:]
        lse_ref[0, t], lse_ref[1, t] = lse[:TOK], lse[TOK:]
        return 0

    lax.fori_loop(0, NT, one, 0)


SM = pl.BlockSpec(memory_space=pltpu.SMEM)


def attend(x_index, q, k, v, start):
    return pl.pallas_call(
        attend_kernel,
        out_shape=(
            jax.ShapeDtypeStruct((2, NT, TOK, HD), F32),
            jax.ShapeDtypeStruct((2, NT, TOK, 1), F32),
        ),
        in_specs=[SM, VM, VM, VM, VM],
        out_specs=(VM, VM),
        compiler_params=pltpu.CompilerParams(vmem_limit_bytes=40 * 2**20),
        name="attend",
    )(x_index, q, k, v, start)


def attend_back_kernel(
    x_ref, q_ref, k_ref, v_ref, go_ref, start_ref, lse_ref, delta_ref, gq_ref, gk_ref, gv_ref
):
    x = x_ref[0]
    gk_ref[...] = jnp.zeros_like(gk_ref)
    gv_ref[...] = jnp.zeros_like(gv_ref)

    def tile(t, kt, given, gq, diagonal):
        q, go, start, lse, delta = given
        k, v = keys_of(k_ref, kt), keys_of(v_ref, kt)
        s = mm_nt(k, q)
        place = kt * CHUNK + lax.broadcasted_iota(jnp.int32, (CHUNK, QROWS), 0)
        keep = place >= start
        if diagonal:
            column = lax.broadcasted_iota(jnp.int32, (CHUNK, QROWS), 1)
            query = t * CHUNK + x * TOK + lax.rem(column, TOK)
            keep = keep & (place <= query)
        p = jnp.where(keep, jnp.exp2(s - lse), 0.0)
        gp = mm_nt(v, go)
        gs = (p * (gp - delta)).astype(BF)
        gv = mm(p.astype(BF), go)
        gk = mm(gs, q)
        for n in range(NX):
            rows = slice(n * TOK, (n + 1) * TOK)
            gv_ref[n, kt] += gv[rows]
            gk_ref[n, kt] += gk[rows]
        return gq + mm_tn(gs, k)

    def one(t, _):
        q = jnp.concatenate([q_ref[0, t], q_ref[1, t]], axis=0)
        go = jnp.concatenate([go_ref[0, t], go_ref[1, t]], axis=0)
        start = jnp.concatenate([start_ref[t]] * 2, axis=1)
        lse = jnp.concatenate([lse_ref[0, t], lse_ref[1, t]], axis=1)
        delta = jnp.concatenate([delta_ref[0, t], delta_ref[1, t]], axis=1)
        given = (q, go, start, lse, delta)
        gq = jnp.zeros((QROWS, HD), F32)
        gq = lax.fori_loop(0, t, lambda kt, g: tile(t, kt, given, g, False), gq)
        gq = tile(t, t, given, gq, True) * SCALE
        gq_ref[0, t], gq_ref[1, t] = gq[:TOK], gq[TOK:]
        return 0

    lax.fori_loop(0, NT, one, 0)


def attend_back(x_index, q, k, v, go, start, lse, delta):
    return pl.pallas_call(
        attend_back_kernel,
        out_shape=(
            jax.ShapeDtypeStruct((2, NT, TOK, HD), F32),
            jax.ShapeDtypeStruct((NX, NT, TOK, HD), F32),
            jax.ShapeDtypeStruct((NX, NT, TOK, HD), F32),
        ),
        in_specs=[SM] + [VM] * 7,
        out_specs=(VM, VM, VM),
        compiler_params=pltpu.CompilerParams(vmem_limit_bytes=48 * 2**20),
        name="attend_back",
    )(x_index, q, k, v, go, start, lse, delta)


def turn(v, cosine, sine):
    half = HD // 2
    v1, v2 = v[..., :half], v[..., half:]
    return jnp.concatenate([v1 * cosine - v2 * sine, v2 * cosine + v1 * sine], axis=-1)


def body(
    tokens,
    doc_lengths,
    w_query,
    w_key,
    w_value,
    w_output,
    w_gate,
    w_up,
    w_down,
    gain_attn,
    gain_mlp,
    cotangent,
):
    width = tokens.shape[2]
    rows = w_query.shape[0]
    hidden_width = w_gate.shape[1]
    part = hidden_width // NT
    everyone = ("z", "yl", "c")
    x_index = lax.axis_index("x")
    yl, c, yh = lax.axis_index("yl"), lax.axis_index("c"), lax.axis_index("yh")
    ylc = yl * 2 + c
    x_scalar = x_index.reshape(1)

    wqkv = jnp.concatenate(
        [
            w_query.reshape(rows, NT, 2 * HD),
            w_key.reshape(rows, NT, HD),
            w_value.reshape(rows, NT, HD),
        ],
        axis=2,
    ).transpose(1, 0, 2)

    def hidden_slices(w):
        w = w.reshape(rows, 4, 4, 2, TOK).transpose(2, 3, 0, 1, 4)
        return w.reshape(NT, rows, part)

    wgu = jnp.concatenate([hidden_slices(w_gate), hidden_slices(w_up)], axis=2)
    down_own = lax.dynamic_slice_in_dim(w_down, yh * TOK, TOK, 0)
    gains = lax.all_gather(jnp.stack([gain_attn, gain_mlp], axis=1), everyone, axis=0, tiled=True)
    gains = gains.astype(F32)
    g1, g2 = gains[:, 0][None, :], gains[:, 1][None, :]
    tok_all, qkv_part, gu_part, o_half = first_gather(tokens[0], wqkv, wgu, w_output)
    qkv_w = lax.all_gather(qkv_part, "z", axis=0, tiled=True).reshape(width, 4 * HD)
    gu_w = lax.all_gather(gu_part, "z", axis=0, tiled=True).reshape(width, 2 * part)
    down_w = lax.all_gather(down_own, "z", axis=0, tiled=True)
    o_w = lax.all_gather(o_half, ("z", "c"), axis=0)
    o_w = o_w.reshape((4, 2) + o_half.shape).transpose(0, 2, 1, 3, 4).reshape(width, width)
    cot_all = lax.all_gather(cotangent[0], GROUP, axis=0, tiled=True)

    lengths = doc_lengths[0]
    places = (
        jnp.arange(NT, dtype=jnp.int32)[:, None] * CHUNK
        + x_index * TOK
        + jnp.arange(TOK, dtype=jnp.int32)[None, :]
    ).reshape(-1)
    segment, start = doc_layout(lengths, places)
    valid = (segment < lengths.shape[0]).astype(F32)[:, None]
    angles = (places - start).astype(F32)[:, None] * jnp.asarray(frequency_table(HD))[None, :]
    cosine, sine = jnp.cos(angles), jnp.sin(angles)
    start = start.reshape(NT, TOK)

    x_all = tok_all.reshape(NT * TOK, width).astype(F32)
    h1 = x_all * lax.rsqrt(jnp.mean(x_all * x_all, axis=1, keepdims=True) + NORM_EPS)
    h1 = (h1 * g1).astype(BF)
    qkv = mm(h1, qkv_w)
    q = turn(qkv[:, : 2 * HD].reshape(-1, 2, HD), cosine[:, None], sine[:, None])
    q = (q * (SCALE * LOG2E)).astype(BF).transpose(1, 0, 2).reshape(2, NT, TOK, HD)
    k = turn(qkv[:, 2 * HD : 3 * HD], cosine, sine).astype(BF).reshape(NT, TOK, HD)
    v = qkv[:, 3 * HD :].astype(BF).reshape(NT, TOK, HD)
    kv = lax.all_gather(jnp.stack([k, v]), "x", axis=0)
    k_all, v_all = kv[:, 0], kv[:, 1]
    attended, lse = attend(x_scalar, q, k_all, v_all, start[..., None])
    flat = attended.transpose(1, 2, 0, 3).reshape(NT * TOK, 2 * HD)
    ob = (flat * valid).astype(BF)
    ob_all = gather_group(ob, "gather_ob", 1)
    ob_all = ob_all.transpose(1, 0, 2).reshape(NT * TOK, width)

    x2 = x_all + mm(ob_all, o_w)
    r2 = lax.rsqrt(jnp.mean(x2 * x2, axis=1, keepdims=True) + NORM_EPS)
    h2 = (x2 * r2 * g2).astype(BF)
    gu = mm(h2, gu_w)
    gate, up = gu[:, :part], gu[:, part:]
    sigmoid = jax.nn.sigmoid(gate)
    silu = gate * sigmoid
    hidden = (silu * up).astype(BF)
    y_part = mm(hidden, down_w).astype(BF).reshape(NT, TOK, width)
    gh = mm_nt(cot_all, down_w)
    ggate = (gh * up * sigmoid * (1.0 + gate * (1.0 - sigmoid))).astype(BF)
    gup = (gh * silu).astype(BF)
    ggu = jnp.concatenate([ggate, gup], axis=1)
    gh2_part = mm_nt(ggu, gu_w).astype(BF).reshape(NT, TOK, width)
    gh2 = scatter_group(gh2_part, "scatter_gh2", 2)
    t = ylc * 2 + yh
    own = lax.dynamic_slice_in_dim(x2, t * TOK, TOK, 0)
    own_r2 = lax.dynamic_slice_in_dim(r2, t * TOK, TOK, 0)
    n2 = own * own_r2
    gm = gh2 * g2
    gain_mlp_grad = jnp.sum(gh2 * n2, axis=0)
    gx2 = own_r2 * (gm - n2 * jnp.mean(gm * n2, axis=1, keepdims=True)) + cotangent[0].astype(F32)
    ga = gather_group(gx2.astype(BF), "gather_ga", 3).reshape(NT * TOK, width)
    layer_out = own + scatter_group(y_part, "scatter_y", 4)

    o_rows = lax.dynamic_slice_in_dim(o_w, t * 2 * HD, 2 * HD, 0)
    go = (mm_nt(ga, o_rows) * valid).astype(BF)
    delta = jnp.sum((go.astype(F32) * flat).reshape(NT, TOK, 2, HD), axis=3)
    delta = delta.transpose(2, 0, 1)[:, :, None, :]
    go4 = go.reshape(NT, TOK, 2, HD).transpose(2, 0, 1, 3)
    gq, gk, gv = attend_back(
        x_scalar, q, k_all, v_all, go4, start[:, None, :], lse.transpose(0, 1, 3, 2), delta
    )
    gkv = jnp.stack([gk * LN2, gv], axis=1).astype(BF)
    gkv = lax.psum_scatter(gkv, "x", scatter_dimension=0).astype(F32)
    gq = turn(gq.transpose(1, 2, 0, 3).reshape(-1, 2, HD), cosine[:, None], -sine[:, None])
    gk = turn(gkv[0].reshape(-1, HD), cosine, -sine)
    gqkv = jnp.concatenate([gq.reshape(-1, 2 * HD), gk, gkv[1].reshape(-1, HD)], axis=1).astype(BF)
    gh1_part = mm_nt(gqkv, qkv_w).astype(BF).reshape(NT, TOK, width)
    gh1 = scatter_group(gh1_part, "scatter_gh1", 5)
    x_own = tokens[0].astype(F32)
    r1 = lax.rsqrt(jnp.mean(x_own * x_own, axis=1, keepdims=True) + NORM_EPS)
    n1 = x_own * r1
    gn = gh1 * g1
    gain_attn_grad = jnp.sum(gh1 * n1, axis=0)
    tokens_grad = gx2 + r1 * (gn - n1 * jnp.mean(gn * n1, axis=1, keepdims=True))

    ob_heads = ob_all.reshape(NT * TOK, 4, 4, HD)
    ob_mine = lax.dynamic_index_in_dim(ob_heads, ylc, 2, keepdims=False).reshape(NT * TOK, 4 * HD)
    ga_mine = lax.dynamic_slice_in_dim(ga, yh * (width // 2), width // 2, 1)
    grad_o = mm_tn(ob_mine, ga_mine).astype(BF)
    grad_gu = mm_tn(h2, ggu).astype(BF)
    grad_down = mm_tn(hidden, cot_all).astype(BF)
    grad_qkv = mm_tn(h1, gqkv).astype(BF)
    gain_grads = jnp.stack([gain_attn_grad, gain_mlp_grad], axis=1).astype(BF)
    gain_grads = jnp.pad(gain_grads, ((0, 0), (0, TOK - 2)))

    def over_z(a):
        return lax.psum_scatter(a, "z", scatter_dimension=0, tiled=True)

    sum_gu, sum_down, sum_o = over_z(grad_gu), over_z(grad_down), over_z(grad_o)
    sum_qkv = over_z(jnp.concatenate([grad_qkv, gain_grads], axis=1))
    columns = jnp.concatenate([sum_gu, sum_qkv], axis=1)
    columns = lax.all_to_all(columns, ("yl", "c"), split_axis=0, concat_axis=0, tiled=True)
    columns, sum_down, sum_o = lax.psum((columns, sum_down, sum_o), "x")
    columns = lax.all_gather(columns, "yh", axis=0)
    sum_down = lax.all_gather(sum_down, "yh", axis=0, tiled=True).astype(F32)
    sum_o = lax.all_gather(sum_o, "yh", axis=1, tiled=True).astype(F32)
    columns = columns.reshape(2, 4, rows, 2 * part + 4 * TOK).astype(F32)
    columns = columns.transpose(2, 1, 0, 3)

    def hidden_columns(a):
        return a.reshape(rows, 4, 2, 4, TOK).transpose(0, 3, 1, 2, 4).reshape(rows, hidden_width)

    grad_gate = hidden_columns(columns[..., :part])
    grad_up = hidden_columns(columns[..., part : 2 * part])
    base = 2 * part
    grad_query = columns[..., base : base + 2 * HD].reshape(rows, width)
    grad_key = columns[..., base + 2 * HD : base + 3 * HD].reshape(rows, KV * HD)
    grad_value = columns[..., base + 3 * HD : base + 4 * HD].reshape(rows, KV * HD)
    grad_gains = jnp.sum(columns[..., base + 4 * HD : base + 4 * HD + 2], axis=(1, 2))
    return (
        layer_out.astype(BF)[None],
        tokens_grad.astype(BF)[None],
        grad_query,
        grad_key,
        grad_value,
        sum_o,
        grad_gate,
        grad_up,
        sum_down,
        grad_gains[:, 0],
        grad_gains[:, 1],
    )


def solution(mesh):
    fine = Mesh(mesh.devices.reshape(4, 2, 2, 2, 4), AXES)
    by_token = P("z", ("yl", "c", "yh", "x"), None)
    by_row = P(("z", "yl", "c"), None)
    by_feature = P(("z", "yl", "c"))
    return jax.shard_map(
        body,
        mesh=fine,
        in_specs=(by_token, P("z", None))
        + (by_row,) * 7
        + (by_feature, by_feature, by_token),
        out_specs=(by_token, by_token) + (by_row,) * 7 + (by_feature, by_feature),
        check_vma=False,
    )
```

time: 1280 us -> 707 us (0.55)
  waiting for transfers between devices: 838 us -> 258 us
  Pallas kernels: 0 us -> 207 us
  matrix products: 196 us -> 62.1 us
  starting transfers between devices: 44.9 us -> 6.07 us
    reduce_scatter x3 -> x5, waiting for transfers between devices: 475 us -> 83.4 us  [the longest x4 75.2 us: over_z(): return lax.psum_scatter(a, 'z', scatter_dimension=0, tiled=True)]
    pallas_call x0 -> x8, Pallas kernels: none -> 207 us  [the longest x3 91.4 us: scatter_group(): pl.pallas_call(scatter_kernel, out_shape=jax.ShapeDtypeStruct((rows, widt...]
    all_gather x8 -> x7, waiting for transfers between devices: 264 us -> 118 us  [the longest x1 74.4 us: body(): cot_all = lax.all_gather(cotangent[0], GROUP, axis=0, tiled=True)]
    dot_general x49 -> x12, matrix products: 196 us -> 62.1 us  [the longest x4 24.1 us: mm(): return jnp.dot(a, b, preferred_element_type=F32)]
    all_to_all x5 -> x1, starting transfers between devices: 44 us -> 5.37 us  [body(): lax.all_to_all(columns, ('yl', 'c'), split_axis=0, concat_axis=0, tiled=T...]
    psum x1, waiting for transfers between devices: 88.6 us -> 54.1 us  [body(): columns, sum_down, sum_o = lax.psum((columns, sum_down, sum_o), 'x')]
    all_gather x0 -> x3, blocking collectives: none -> 34.2 us  [the longest x1 19 us: body(): lax.all_gather(jnp.stack([gain_attn, gain_mlp], axis=1), everyone, axis=0...]
    reshape x2 -> x21, local copies, waits for them, and re-layouts: 1.33 us -> 28.2 us  [the longest x4 10.2 us: hidden_columns(): a.reshape(rows, 4, 2, 4, TOK).transpose(0, 3, 1, 2, 4)]
  transfers between devices with their start and end apart: 17 -> 14, of which waited for: 12 -> 11; matrix products, arithmetic and copies ran while one was open for 15% -> 14% of each run, Pallas kernels for 0% -> 16%
where the time goes in v1:
time: 707 us; the launch traced here: 698 us
  waiting for transfers between devices  258 us (36%)
  Pallas kernels  207 us (29%)
  local copies, waits for them, and re-layouts  73.4 us (10%)
  matrix products  62.1 us (9%)
  other arithmetic  42.4 us (6%)
  blocking collectives  34.2 us (5%)
  between operations  15.2 us (2%)
    pallas_call x3, Pallas kernels, scatter_group(): pl.pallas_call(scatter_kernel, out_shape=jax.ShapeDtypeStruct((rows, widt...  91.4 us
    reduce_scatter x4, waiting for transfers between devices, over_z(): return lax.psum_scatter(a, 'z', scatter_dimension=0, tiled=True)  75.2 us
    all_gather x1, waiting for transfers between devices, body(): cot_all = lax.all_gather(cotangent[0], GROUP, axis=0, tiled=True)  74.4 us
    psum x1, waiting for transfers between devices, body(): columns, sum_down, sum_o = lax.psum((columns, sum_down, sum_o), 'x')  54.1 us
    pallas_call x2, Pallas kernels, gather_group(): pl.pallas_call(gather_kernel, out_shape=jax.ShapeDtypeStruct((NT, rows, w...  43.8 us
    pallas_call x1, Pallas kernels, first_gather(): pl.pallas_call(first_kernel, out_shape=(like((NT,) + tok.shape), like((4,...  31.2 us
    dot_general x4, matrix products, mm(): return jnp.dot(a, b, preferred_element_type=F32)  24.1 us
    all_gather x1, waiting for transfers between devices, body(): kv = lax.all_gather(jnp.stack([k, v]), 'x', axis=0)  23.4 us
  transfers between devices with their start and end apart: 14, of which 11 were waited for; matrix products, arithmetic and copies ran while one was open for 14% of the time, Pallas kernels for 16%

profile of v1, /device:TPU:27, one launch (start us, length us, event | category | flops | bytes accessed | tf_op | source)
XLA Modules:
  0.0 698.0 jit_solution(16006891298987989333)
XLA Ops:
  19.4 31.2 %first_gather.1 = (bf16[8,128,1536]{2,1,0:T(8,128)(2,1)}, bf16[4,96,384]{2,1,0:T(8,128)(2,1)}, bf16[4,96,1024]{2,1,0:T(8,128)(2,1)}, bf16[2,96,1536]{2,1,0:T(8,1...) custom-call(bf16[128,1536]{1,0:T(8,128)(2,1)} %bitcast.218, bf16[8,96,384]{2,1,0:T(8,128)(2,1)} %maximum_bitcast_fusion.wqkv, ...), custom_call_target="tpu_custom_call" | custom-call | tf_op jit(solution)/shard_map/first_gather/pallas_call | solution.py:299
  50.8 19.0 %all-gather.3 = bf16[16,96,2]{1,2,0:T(2,128)(2,1)S(1)} all-gather(bf16[1,96,2]{1,2,0:T(2,128)(2,1)S(1)} %maximum_bitcast_fusion.1), channel_id=1, replica_groups=mesh['z'=4,'yl'=2,'c'=2,'yh'=2,'x'=4] {'z','yl','c'}, dimensions={0}, use_global_device_ids=true | all-gather | bytes 6528 | tf_op jit(solution)/shard_map/all_gather | solution.py:489
  77.1 3.7 fusion.73
  86.9 23.4 %all-gather.20.cloned.1.call-done = bf16[8,8,128,96]{2,3,1,0:T(8,128)(2,1)} async-done(((bf16[2,8,128,96]{2,3,1,0:T(8,128)(2,1)}), bf16[8,8,128,96]{2,3,1,0:T(8,128)(2,1)}) %all-gather.20.cloned.1.call-update) | async-done | bytes 1572880 | tf_op jit(solution)/shard_map/all_gather | solution.py:520
  115.4 17.7 %attend.1 = (f32[2,8,128,96]{3,2,1,0:T(8,128)S(1)}, f32[2,8,128,1]{3,2,1,0:T(8,128)S(1)}) custom-call(s32[1]{0:T(128)} %bitcast.5.x_ref, bf16[2,8,128,96]{3,2,1,0:T(8,128)(2,1)S(1)} %bitcast.201, bf16[4,8,128,96]{3,2,1,0:T(8,128)(2,1)S(1)} %bitcast.199, bf16[4,8,128,96]{3,2,1,0:T(8,128)(2,1)S(1)} %bitcast.197, s32[8,128,1]{2,1,0:T(8,128)S(1)} %copy.236.start_ref), custom_call_target="tpu_custom_call" | custom-call | tf_op jit(solution)/shard_map/attend/pallas_call | solution.py:372
  142.6 24.6 %gather_ob.1 = bf16[8,1024,192]{2,1,0:T(8,128)(2,1)} custom-call(bf16[1024,192]{1,0:T(8,128)(2,1)} %multiply_convert_fusion.3.own), custom_call_target="tpu_custom_call" | custom-call | tf_op jit(solution)/shard_map/gather_ob/pallas_call | solution.py:175
  167.2 6.2 copy.240
  180.6 7.6 %multiply_reduce_fusion = (f32[1024]{0:T(1024)S(1)}, f32[1024,1536]{1,0:T(8,128)}) fusion(bf16[1024,1536]{0,1:T(8,128)(2,1)S(1)} %bitcast.220, bf16[1536,1536]{1,0:T(8,128)(2,1)S(1)} %bitcast.222, bf16[8,128,1536]{2,1,0:T(8,128)(2,1)S(1)} %copy-done.8), kind=kOutput, calls=%fused_computation.10 | convolution fusion | flops 4838128640 | bytes 17305600 | tf_op jit(solution)/shard_map/dot_general | solution.py:54
  188.9 9.3 %fusion.68 = f32[1024,1024]{0,1:T(8,128)} fusion(bf16[1536,1024]{1,0:T(8,128)(2,1)} %bitcast.249, f32[1024,1536]{1,0:T(8,128)} %get-tuple-element.73, f32[1536]{0:T(1024)S(1)} %get-tuple-element.35, f32[1024]{0:T(1024)S(1)} %add_rsqrt_fusion), kind=kOutput, calls=%fused_computation.139 | convolution fusion | flops 3225944064 | bytes 13641728 | tf_op jit(solution)/shard_map/dot_general | solution.py:54
  198.2 19.5 %all-gather.16.cloned.1.call-done = bf16[512,1536]{1,0:T(8,128)(2,1)} async-done(((bf16[128,1536]{1,0:T(8,128)(2,1)}), bf16[512,1536]{1,0:T(8,128)(2,1)}) %all-gather.16.cloned.1.call-update) | async-done | bytes 1572880 | tf_op jit(solution)/shard_map/all_gather | solution.py:495
  217.8 74.4 %all-gather.24.cloned.1.call-done = bf16[1,1024,1536]{2,1,0:T(8,128)(2,1)} async-done(((bf16[1,128,1536]{2,1,0:T(8,128)(2,1)}), bf16[1,1024,1536]{2,1,0:T(8,128)(2,1)}) %all-gather.24.cloned.1.call-update) | async-done | bytes 3145744 | tf_op jit(solution)/shard_map/all_gather | solution.py:498
  292.2 7.2 %fusion.15 = (bf16[1024,512]{0,1:T(8,128)(2,1)S(1)}, bf16[1024,512]{0,1:T(8,128)(2,1)S(1)}, bf16[1024,512]{0,1:T(8,128)(2,1)}) fusion(f32[1024,1024]{0,1:T(8,128)} %fusion.68, bf16[512,1536]{1,0:T(8,128)(2,1)} %all-gather.16.cloned.1.call-done, bf16[1,1024,1536]{2,1,0:T(8,128)(2,1)} %all-gather.24.cloned.1.call-done), kind=kOutput, calls=%fused_computation.30 | convolution fusion | flops 1618477056 | bytes 12058624 | tf_op jit(solution)/shard_map/dot_general | solution.py:58
  299.4 3.9 convolution_convert_fusion.3
  303.4 22.6 %scatter_gh2.1 = f32[128,1536]{1,0:T(8,128)S(1)} custom-call(bf16[8,128,1536]{2,1,0:T(8,128)(2,1)S(1)} %bitcast.205), custom_call_target="tpu_custom_call" | custom-call | tf_op jit(solution)/shard_map/scatter_gh2/pallas_call | solution.py:234
  329.6 19.2 %gather_ga.1 = bf16[8,128,1536]{2,1,0:T(8,128)(2,1)} custom-call(bf16[128,1536]{1,0:T(8,128)(2,1)} %fusion.67.own), custom_call_target="tpu_custom_call" | custom-call | tf_op jit(solution)/shard_map/gather_ga/pallas_call | solution.py:175
  358.5 22.8 %attend_back.1 = (f32[2,8,128,96]{3,2,1,0:T(8,128)S(1)}, f32[4,8,128,96]{3,2,1,0:T(8,128)}, f32[4,8,128,96]{3,2,1,0:T(8,128)}) custom-call(s32[1]{0:T(128)} %bitcast.5.x_ref, bf16[2,8,128,96]{3,2,1,0:T(8,128)(2,1)S(1)} %bitcast.202, bf16[4,8,128,96]{3,2,1,0:T(8,128)(2,1)S(1)} %bitcast.200, bf16[4,8,128,96]{3,2,1,0:T(8,128)(2,1)S(1)} %bitcast.198, ...), custom_call_target="tpu_custom_call" | custom-call | tf_op jit(solution)/shard_map/attend_back/pallas_call | solution.py:430
  387.4 8.8 %convolution_convert_fusion.2 = bf16[1536,1024]{1,0:T(8,128)(2,1)} fusion(bf16[1024,512]{0,1:T(8,128)(2,1)} %copy-done.31, bf16[1024,512]{0,1:T(8,128)(2,1)} %copy-done.30, f32[1024,1536]{1,0:T(8,128)} %get-tuple-element.73, f32[1536]{0:T(1024)S(1)} %get-tuple-element.35, f32[1024]{0:T(1024)S(1)} %add_rsqrt_fusion), kind=kOutput, calls=%fused_computation.14 | convolution fusion | flops 3231711232 | bytes 11544576 | tf_op jit(solution)/shard_map/dot_general | solution.py:62
  397.4 4.5 fusion.4
  406.2 8.2 %reduce-scatter.6.cloned.1.call-done = bf16[1,2,8,128,96]{3,4,2,1,0:T(8,128)(2,1)} async-done(((bf16[4,2,8,128,96]{3,4,2,1,0:T(8,128)(2,1)}), bf16[1,2,8,128,96]{3,4,2,1,0:T(8,128)(2,1)}) %reduce-scatter.6.cloned.1.call-update) | async-done | bytes 393232 | tf_op jit(solution)/shard_map/reduce_scatter | solution.py:562
  419.9 19.1 %scatter_gh1.1 = f32[128,1536]{1,0:T(8,128)S(1)} custom-call(bf16[8,128,1536]{2,1,0:T(8,128)(2,1)S(1)} %bitcast.206), custom_call_target="tpu_custom_call" | custom-call | tf_op jit(solution)/shard_map/scatter_gh1/pallas_call | solution.py:234
  439.6 3.8 convolution_convert_fusion.4
  449.2 4.9 fusion.10
  456.6 27.7 %reduce-scatter.10.cloned.1.call-done = bf16[384,512]{1,0:T(8,128)(2,1)} async-done(((bf16[1536,512]{1,0:T(8,128)(2,1)}), bf16[384,512]{1,0:T(8,128)(2,1)}) %reduce-scatter.10.cloned.1.call-update) | async-done | bytes 393232 | tf_op jit(solution)/shard_map/reduce_scatter | solution.py:586
  486.7 5.4 all-to-all-start
  492.0 15.6 %reduce-scatter.12.cloned.1.call-done = bf16[96,768]{1,0:T(8,128)(2,1)} async-done(((bf16[384,768]{1,0:T(8,128)(2,1)}), bf16[96,768]{1,0:T(8,128)(2,1)}) %reduce-scatter.12.cloned.1.call-update) | async-done | bytes 147472 | tf_op jit(solution)/shard_map/reduce_scatter | solution.py:586
  507.6 29.4 %reduce-scatter.14.cloned.1.call-done = bf16[128,1536]{1,0:T(8,128)(2,1)} async-done(((bf16[512,1536]{1,0:T(8,128)(2,1)}), bf16[128,1536]{1,0:T(8,128)(2,1)}) %reduce-scatter.14.cloned.1.call-update) | async-done | bytes 393232 | tf_op jit(solution)/shard_map/reduce_scatter | solution.py:586
  538.1 54.1 %all-reduce.4.cloned.1.call-done = (bf16[1,384,1536]{2,1,0:T(8,128)(2,1)}, bf16[96,768]{1,0:T(8,128)(2,1)}, bf16[128,1536]{1,0:T(8,128)(2,1)}) async-done(((bf16[1,384,1536]{2,1,0:T(8,128)(2,1)}, bf16[96,768]{1,0:T(8,128)(2,1)}, bf16[128,1536]{1,0:T(8,128)(2,1)}), (bf16[1,384,1536]{2,1,0:T(8,128)(2,1)}, bf16[96,768]{1,0:T(8,128)(2,1)}, bf16[128,1536]{1,0:T(8,128)(2,1)})) %all-reduce.4.cloned.1.call-update) | async-done | bytes 1720336 | tf_op jit(solution)/shard_map/psum | solution.py:592
  592.2 3.6 convolution_convert_fusion.1
  595.8 49.7 %scatter_y.1 = f32[128,1536]{1,0:T(8,128)S(1)} custom-call(bf16[8,128,1536]{2,1,0:T(8,128)(2,1)S(1)} %bitcast.204), custom_call_target="tpu_custom_call" | custom-call | tf_op jit(solution)/shard_map/scatter_y/pallas_call | solution.py:234
  648.0 6.2 all_gather.50
  655.0 9.0 %all_gather.51 = bf16[256,1536]{1,0:T(8,128)(2,1)S(1)} all-gather(bf16[128,1536]{1,0:T(8,128)(2,1)S(1)} %copy-done.22), channel_id=1, replica_groups=mesh['z'=4,'yl'=2,'c'=2,'yh'=2,'x'=4] {'yh'}, dimensions={0}, use_global_device_ids=true | all-gather | bytes 1179648 | tf_op jit(solution)/shard_map/all_gather | solution.py:594
  677.2 3.3 reshape.447
  (208 shorter events, 117.1 us)
Async XLA Ops:
  7.2 77.5 %copy-start = (bf16[256,1536]{1,0:T(8,128)(2,1)S(1)}, bf16[256,1536]{1,0:T(8,128)(2,1)}, u32[]{:S(2)}) copy-start(bf16[256,1536]{1,0:T(8,128)(2,1)} %param.21) | copy-start | bytes 2359300
  7.2 5.3 copy-start.19
  7.2 69.9 %all-gather.12.cloned.1.call-start = ((), (), s32[]{:S(2)}) async-start(), calls=%async_computation.6 | async-start | bytes 1474560 | tf_op jit(solution)/shard_map/all_gather | solution.py:493
  16.9 33.9 %copy-start.26 = (bf16[96]{0:T(256)(128)(2,1)S(1)}, bf16[96]{0:T(256)(128)(2,1)}, u32[]{:S(2)}) copy-start(bf16[96]{0:T(256)(128)(2,1)} %param.23) | copy-start | bytes 580
  16.9 33.9 %copy-start.27 = (bf16[96]{0:T(256)(128)(2,1)S(1)}, bf16[96]{0:T(256)(128)(2,1)}, u32[]{:S(2)}) copy-start(bf16[96]{0:T(256)(128)(2,1)} %param.22) | copy-start | bytes 580
  16.9 52.9 %copy-start.28 = (s32[1,8]{1,0:T(1,128)S(1)}, s32[1,8]{1,0:T(1,128)}, u32[]{:S(2)}) copy-start(s32[1,8]{1,0:T(1,128)} %param.14) | copy-start | bytes 100
  50.7 59.7 %all-gather.20.cloned.1.call-start = ((), (), s32[]{:S(2)}) async-start(), calls=%async_computation.15 | async-start | bytes 1966080 | tf_op jit(solution)/shard_map/all_gather | solution.py:520
  82.4 4.0 copy-start.17
  83.3 91.8 %all-gather.22.cloned.1.call-start = ((), (), s32[]{:S(2)}) async-start(), calls=%async_computation.16 | async-start | bytes 5308416 | tf_op jit(solution)/shard_map/all_gather | solution.py:496
  84.0 104.8 %all-gather.14.cloned.1.call-start = ((), (), s32[]{:S(2)}) async-start(), calls=%async_computation.7 | async-start | bytes 3932160 | tf_op jit(solution)/shard_map/all_gather | solution.py:494
  84.6 133.2 %all-gather.16.cloned.1.call-start = ((), (), s32[]{:S(2)}) async-start(), calls=%async_computation.8 | async-start | bytes 1966080 | tf_op jit(solution)/shard_map/all_gather | solution.py:495
  85.5 206.7 %all-gather.24.cloned.1.call-start = ((), (), s32[]{:S(2)}) async-start(), calls=%async_computation.17 | async-start | bytes 3538944 | tf_op jit(solution)/shard_map/all_gather | solution.py:498
  86.0 328.4 %reduce-scatter.6.cloned.1.call-start = ((), (), s32[]{:S(2)}) async-start(), calls=%async_computation.9 | async-start | bytes 1966080 | tf_op jit(solution)/shard_map/reduce_scatter | solution.py:562
  136.8 30.5 %copy-start.9 = (f32[8,128,2,96]{1,0,3,2:T(8,128)}, f32[8,128,2,96]{1,0,3,2:T(8,128)S(1)}, u32[]{:S(2)}) copy-start(f32[8,128,2,96]{1,0,3,2:T(8,128)S(1)} %copy.237) | copy-start | bytes 2359300
  175.1 5.6 copy-start.12
  177.9 10.3 %copy-start.13 = (bf16[4,2,2,96,1536]{4,3,2,1,0:T(8,128)(2,1)}, bf16[4,2,2,96,1536]{4,3,2,1,0:T(8,128)(2,1)S(1)}, u32[]{:S(2)}) copy-start(bf16[4,2,2,96,1536]{4,3,2,1,0:T(8,128)(2,1)S(1)} %copy.241) | copy-start | bytes 14155780
  292.2 7.2 %copy-start.25 = (bf16[16,96,1024]{2,1,0:T(8,128)(2,1)S(1)}, bf16[16,96,1024]{2,1,0:T(8,128)(2,1)}, u32[]{:S(2)}) copy-start(bf16[16,96,1024]{2,1,0:T(8,128)(2,1)} %all-gather.14.cloned.1.call-done) | copy-start | bytes 9437188
  299.4 4.0 copy-start.30
  299.4 4.0 copy-start.31
  303.4 24.0 %copy-start.15 = (bf16[1,128,1536]{2,1,0:T(8,128)(2,1)S(1)}, bf16[1,128,1536]{2,1,0:T(8,128)(2,1)}, u32[]{:S(2)}) copy-start(bf16[1,128,1536]{2,1,0:T(8,128)(2,1)} %param.24) | copy-start | bytes 1179652
  387.4 69.3 %reduce-scatter.8.cloned.1.call-start = ((), (), s32[]{:S(2)}) async-start(), calls=%async_computation.10 | async-start | bytes 3932160 | tf_op jit(solution)/shard_map/reduce_scatter | solution.py:586
  396.2 88.1 %reduce-scatter.10.cloned.1.call-start = ((), (), s32[]{:S(2)}) async-start(), calls=%async_computation.11 | async-start | bytes 1966080 | tf_op jit(solution)/shard_map/reduce_scatter | solution.py:586
  397.4 4.6 copy-start.3
  444.7 4.4 copy-start.29
  444.7 62.9 %reduce-scatter.12.cloned.1.call-start = ((), (), s32[]{:S(2)}) async-start(), calls=%async_computation.13 | async-start | bytes 737280 | tf_op jit(solution)/shard_map/reduce_scatter | solution.py:586
  449.1 87.9 %reduce-scatter.14.cloned.1.call-start = ((), (), s32[]{:S(2)}) async-start(), calls=%async_computation.14 | async-start | bytes 1966080 | tf_op jit(solution)/shard_map/reduce_scatter | solution.py:586
  486.7 50.4 %all-to-all-start = ((bf16[4,96,1536]{2,1,0:T(8,128)(2,1)}), bf16[4,96,1536]{2,1,0:T(8,128)(2,1)S(1)}, u32[]{:S(2)}, u32[]{:S(2)}) async-start(bf16[4,96,1536]{2,1,0:T(8,128)(2,1)} %bitcast.52), calls=%async_computation.3 | async-start | bytes 2359296 | tf_op jit(solution)/shard_map/all_to_all | solution.py:591
  492.0 100.1 %all-reduce.4.cloned.1.call-start = ((), (), s32[]{:S(2)}) async-start(), calls=%async_computation.18 | async-start | bytes 3440640 | tf_op jit(solution)/shard_map/psum | solution.py:592
  538.1 127.3 %all-gather.18.cloned.1.call-start = ((), (), s32[]{:S(2)}) async-start(), calls=%async_computation.12 | async-start | bytes 3538944 | tf_op jit(solution)/shard_map/all_gather | solution.py:593
  595.8 49.8 %copy-start.16 = (bf16[1,128,1536]{2,1,0:T(8,128)(2,1)S(1)}, bf16[1,128,1536]{2,1,0:T(8,128)(2,1)}, u32[]{:S(2)}) copy-start(bf16[1,128,1536]{2,1,0:T(8,128)(2,1)} %param.24) | copy-start | bytes 1179652
  645.5 9.5 %copy-start.22 = (bf16[128,1536]{1,0:T(8,128)(2,1)S(1)}, bf16[128,1536]{1,0:T(8,128)(2,1)}, u32[]{:S(2)}) copy-start(bf16[128,1536]{1,0:T(8,128)(2,1)} %get-tuple-element.39) | copy-start | bytes 1179652
  685.3 5.7 copy-start.1
  (14 other events, 30.8 us)
Sparse Core Ops, SparseCore 0:
  50.8 26.2 all-gather.11
  83.4 26.8 all-gather.19
  112.0 36.0 all-gather.21
  149.6 39.1 all-gather.13
  190.9 26.7 all-gather.15
  219.3 72.9 all-gather.23
  387.5 26.9 reduce-scatter.5
  416.9 39.7 reduce-scatter.7
  459.6 24.6 reduce-scatter.9
  487.1 20.4 reduce-scatter.11
  510.6 26.3 reduce-scatter.13
  540.0 52.1 all-reduce.3
  593.9 47.3 all-gather.17

commit v2 on v1

--- a/solution.py
+++ b/solution.py
@@ -64,9 +64,8 @@
 
 class Place:
     def __init__(self):
-        self.yl = lax.axis_index("yl")
-        self.c = lax.axis_index("c")
-        self.yh = lax.axis_index("yh")
+        self.z, self.x = lax.axis_index("z"), lax.axis_index("x")
+        self.yl, self.c, self.yh = (lax.axis_index(name) for name in GROUP)
         self.y = self.yh * 2 + self.yl
         self.t = self.rank(0, self.c)
 
@@ -74,18 +73,31 @@
         y = lax.rem(self.y + (k + 4), 4)
         return lax.rem(y, 2) * 4 + c * 2 + y // 2
 
-    def ring(self, k):
+    def along_y(self, k):
         y = lax.rem(self.y + (k + 4), 4)
         return {"yh": y // 2, "yl": lax.rem(y, 2)}
 
+    def x_at(self, k):
+        return lax.rem(self.x + (k + 4), 4)
+
+    def z_at(self, k):
+        return lax.rem(self.z + (k + 4), 4)
+
+    def along_x(self, k):
+        return {"x": self.x_at(k)}
+
+    def along_z(self, k):
+        return {"z": self.z_at(k)}
+
     def sibling(self):
         return {"c": 1 - self.c}
 
-    def greet(self):
+    def greet(self, others=()):
         barrier = pltpu.get_barrier_semaphore()
-        for who in (self.ring(1), self.ring(-1), self.sibling()):
+        everyone = (self.along_y(1), self.along_y(-1), self.sibling()) + tuple(others)
+        for who in everyone:
             pl.semaphore_signal(barrier, inc=1, device_id=who, device_id_type=MESH)
-        pl.semaphore_wait(barrier, 3)
+        pl.semaphore_wait(barrier, len(everyone))
 
 
 class Sent:
@@ -102,12 +114,12 @@
 
 
 class Copies:
-    def __init__(self, send_sem, recv_sem):
-        self.send_sem, self.recv_sem, self.n, self.all = send_sem, recv_sem, 0, []
+    def __init__(self, send_sem, recv_sem, local_sem=None):
+        self.send_sem, self.recv_sem, self.local_sem = send_sem, recv_sem, local_sem
+        self.all, self.locals = [], []
 
     def __call__(self, src, dst, who):
-        i = self.n
-        self.n += 1
+        i = len(self.all)
         copy = pltpu.make_async_remote_copy(
             src_ref=src,
             dst_ref=dst,
@@ -121,6 +133,12 @@
         self.all.append(sent)
         return sent
 
+    def local(self, src, dst):
+        copy = pltpu.make_async_copy(src, dst, self.local_sem.at[len(self.locals)])
+        copy.start()
+        self.locals.append(copy)
+        return copy
+
     def finish(self):
         for sent in self.all:
             sent.wait_recv()
@@ -128,10 +146,351 @@
             sent.wait_send()
 
 
+class Gather:
+    def __init__(self, send, along, slot, cut, src=None):
+        self.send, self.along, self.slot, self.cut = send, along, slot, cut
+        src = slot(0) if src is None else src
+        self.up = send(src, slot(0), along(1))
+        self.down = send(src, slot(0), along(-1))
+
+    def forward(self):
+        self.up.wait_recv()
+        part = self.cut(self.slot(-1), 0)
+        self.far_up = self.send(part, part, self.along(1))
+        self.down.wait_recv()
+        part = self.cut(self.slot(1), 1)
+        self.far_down = self.send(part, part, self.along(-1))
+
+    def end(self):
+        self.far_up.wait_recv()
+        self.far_down.wait_recv()
+
+
+def halves(ref, i):
+    half = ref.shape[0] // 2
+    return ref.at[pl.ds(i * half, half)]
+
+
+ANY = pl.BlockSpec(memory_space=pl.ANY)
+VM = pl.BlockSpec(memory_space=pltpu.VMEM)
+SM = pl.BlockSpec(memory_space=pltpu.SMEM)
+GROUP_ROWS = NT * TOK
+QROWS = 2 * TOK
+CHUNK = NX * TOK
+PACKED = GROUP_ROWS + GROUP_ROWS // 2
+
+
+def starts_of(lengths_ref, place):
+    end, start = 0, jnp.zeros_like(place)
+    for i in range(lengths_ref.shape[1]):
+        end = end + lengths_ref[0, i]
+        start = jnp.maximum(start, jnp.where(place >= end, end, 0))
+    return start, end
+
+
+def places_of(me, tile, shape, axis):
+    row = lax.broadcasted_iota(jnp.int32, shape, axis)
+    return (tile + row // TOK) * CHUNK + me.x * TOK + lax.rem(row, TOK)
+
+
+def turn(v, cosine, sine):
+    half = HD // 2
+    return v * cosine + jnp.concatenate([-v[:, half:], v[:, :half]], axis=1) * sine
+
+
+def unpack(packed, n):
+    low, high = packed[n:, : TOK // 2], packed[n:, TOK // 2 :]
+    tail = jnp.concatenate([low, high], axis=0)
+    return jnp.concatenate([packed[:n], tail, jnp.zeros_like(tail)], axis=1)
+
+
+def front_kernel(
+    lengths, freq, tok, cot, wq, wk, wv, wg, wu, wo, wd, gain1, gain2,
+    tok_all, cot_all, h1_out, gu_w, o_w, down_w, kv_out, q_out, o_out, lse_out, ob_out, gains_out, qkv_w,
+    tokv, h1, slices_q, slices_u, tmp_q, tmp_u, gq, kv, keyv, starts, top, total, acc,
+    send_sem, recv_sem, local_sem,
+):
+    me = Place()
+    me.greet((me.along_x(1), me.along_x(-1), me.along_z(1), me.along_z(-1)))
+    send = Copies(send_sem, recv_sem, local_sem)
+    c, other = me.c, 1 - me.c
+    step = 1 - 2 * c
+    slot, slot_other = me.yl * 2 + c, me.yl * 2 + other
+    toward, away = me.along_y(step), me.along_y(-step)
+    t_toward, t_relay, t_sib = me.rank(step, c), me.rank(step, other), me.rank(0, other)
+    rows, width = wq.shape
+
+    slices_q[:, rows:, :] = jnp.zeros_like(slices_q[:, rows:, :])
+    for t in range(NT):
+        slices_q[t, :rows] = jnp.concatenate(
+            [
+                wq[:, 2 * HD * t : 2 * HD * (t + 1)],
+                wk[:, HD * t : HD * (t + 1)],
+                wv[:, HD * t : HD * (t + 1)],
+            ],
+            axis=1,
+        )
+        slices_q[t, rows : rows + 1, :rows] = gain1[...]
+        slices_q[t, rows + 1 : rows + 2, :rows] = gain2[...]
+    relay_q = send(slices_q.at[t_relay], tmp_q, me.sibling())
+    arrived_q = [
+        send(slices_q.at[t_sib], gq.at[me.z, slot], me.sibling()),
+        send(slices_q.at[t_toward], gq.at[me.z, slot], toward),
+    ]
+    own_q = send.local(slices_q.at[me.t], gq.at[me.z, slot])
+    own_tok = send.local(tok, tokv.at[me.t])
+    tokens = Gather(send, me.along_y, lambda k: tokv.at[me.rank(k, c)], halves, tok)
+    tok_sib = [send(tok, tokv.at[me.t], me.sibling())]
+    quarter = 32
+    rows_of = lambda i: pl.ds(pl.multiple_of(i * quarter, quarter), quarter)
+    down_src = wd.at[pl.ds(pl.multiple_of(me.yh * TOK + me.x * quarter, quarter), quarter)]
+    own_down = send.local(down_src, down_w.at[me.z, rows_of(me.x)])
+    down_z = Gather(
+        send, me.along_z, lambda k: down_w.at[me.z_at(k), rows_of(me.x)], halves, down_src
+    )
+    relay_q.wait_recv()
+    arrived_q.append(send(tmp_q, gq.at[me.z, slot_other], away))
+
+    part = wg.shape[1] // NT
+    for t in range(NT):
+        for n in range(4):
+            at = n * 2 * CHUNK + t * TOK
+            slices_u[t, :, n * TOK : (n + 1) * TOK] = wg[:, at : at + TOK]
+            slices_u[t, :, part + n * TOK : part + (n + 1) * TOK] = wu[:, at : at + TOK]
+
+    for t in range(NT):
+        place = places_of(me, t, (TOK, TOK), 0)
+        starts[t], _ = starts_of(lengths, place)
+
+    own_q.wait()
+    for copy in arrived_q:
+        copy.wait_recv()
+    qkv_z = Gather(send, me.along_z, lambda k: gq.at[me.z_at(k)], halves)
+    tokens.forward()
+    tok_sib += [
+        send(tokv.at[me.rank(k, c)], tokv.at[me.rank(k, c)], me.sibling()) for k in (-1, 1)
+    ]
+    relay_u = send(slices_u.at[t_relay], tmp_u, me.sibling())
+    arrived_u = [
+        send(slices_u.at[t_sib], gu_w.at[me.z, slot], me.sibling()),
+        send(slices_u.at[t_toward], gu_w.at[me.z, slot], toward),
+    ]
+    own_u = send.local(slices_u.at[me.t], gu_w.at[me.z, slot])
+    third = pl.ds(pl.multiple_of(me.x * CHUNK * 3 // 4, TOK), CHUNK * 3 // 4)
+    arrived_o = send(wo, o_w.at[me.z, me.yl, c], toward)
+    own_o = send.local(wo, o_w.at[me.z, me.yl, c])
+    relay_u.wait_recv()
+    arrived_u.append(send(tmp_u, gu_w.at[me.z, slot_other], away))
+    own_down.wait()
+    down_z.forward()
+    qkv_z.forward()
+    tokens.end()
+    far = tokv.at[me.rank(2, c)]
+    tok_sib.append(send(far, far, me.sibling()))
+    cots = Gather(send, me.along_y, lambda k: cot_all.at[me.rank(k, c)], halves, cot)
+    own_cot = send.local(cot, cot_all.at[me.t])
+    cot_sib = [send(cot, cot_all.at[me.t], me.sibling())]
+    down_z.end()
+    down_x = Gather(
+        send, me.along_x, lambda k: down_w.at[:, rows_of(me.x_at(k))], halves
+    )
+    own_u.wait()
+    for copy in arrived_u:
+        copy.wait_recv()
+    qkv_z.end()
+    gu_z = Gather(send, me.along_z, lambda k: gu_w.at[me.z_at(k)], halves)
+    own_o.wait()
+    arrived_o.wait_recv()
+    o_z = Gather(send, me.along_z, lambda k: o_w.at[me.z_at(k), :, c, :, third], halves)
+    own_tok.wait()
+    for copy in tok_sib:
+        copy.wait_recv()
+    tok_out = send.local(tokv, tok_all)
+
+    gains = [
+        jnp.concatenate(
+            [gq[z, n, rows + g : rows + g + 1, :rows] for z in range(4) for n in range(4)], axis=1
+        ).astype(F32)
+        for g in range(2)
+    ]
+    gains_out[...] = jnp.concatenate(gains, axis=0)
+    for z in range(4):
+        for n in range(4):
+            at = (z * 4 + n) * rows
+            qkv_w[at : at + rows] = gq[z, n, :rows]
+    tails = []
+    for i in range(4):
+        place = places_of(me, 2 * i, (QROWS, HD), 0)
+        start, _ = starts_of(lengths, place)
+        angle = (place - start).astype(F32) * freq[...]
+        cosine, sine = jnp.cos(angle), jnp.sin(angle)
+        x = jnp.concatenate([tokv[2 * i], tokv[2 * i + 1]], axis=0).astype(F32)
+        h = x * lax.rsqrt(jnp.mean(x * x, axis=1, keepdims=True) + NORM_EPS)
+        h = (h * gains[0]).astype(BF)
+        h1[2 * i], h1[2 * i + 1] = h[:TOK], h[TOK:]
+        qkv = mm(h, qkv_w[...])
+        blank = jnp.zeros((QROWS, TOK - HD), BF)
+        for n in range(2):
+            q = turn(qkv[:, n * HD : (n + 1) * HD], cosine, sine) * (SCALE * LOG2E)
+            q = jnp.concatenate([q.astype(BF), blank], axis=1)
+            q_out[2 * i, n * TOK : (n + 1) * TOK] = q[:TOK]
+            q_out[2 * i + 1, n * TOK : (n + 1) * TOK] = q[TOK:]
+        k = turn(qkv[:, 2 * HD : 3 * HD], cosine, sine)
+        kv[me.x, i * QROWS : (i + 1) * QROWS] = jnp.concatenate(
+            [k, qkv[:, 3 * HD : 3 * HD + TOK - HD]], axis=1
+        ).astype(BF)
+        tails.append(qkv[:, 3 * HD + TOK - HD :].astype(BF))
+    for i in range(2):
+        at = GROUP_ROWS + i * QROWS
+        kv[me.x, at : at + QROWS] = jnp.concatenate([tails[i], tails[i + 2]], axis=1)
+    kvs = Gather(send, me.along_x, lambda k: kv.at[me.x_at(k)], halves)
+    h1_copy = send.local(h1, h1_out)
+
+    top[...] = jnp.full_like(top, -1e30)
+    total[...] = jnp.zeros_like(total)
+    acc[...] = jnp.zeros_like(acc)
+
+    def source(s):
+        x = lax.rem(me.x + s + s // 2 - 2 * (s // 3), 4)
+        keyv[...] = unpack(kv[x], GROUP_ROWS)
+        lane = lax.broadcasted_iota(jnp.int32, (QROWS, TOK), 1)
+        for t in range(NT):
+            n = (t + 1) * TOK
+            q = q_out[t]
+            score = mm_nt(q, keyv[:n, :TOK])
+            start = jnp.concatenate([starts[t]] * 2, axis=0)
+            kept = []
+            for b in range(t + 1):
+                key = lane + (b * CHUNK + x * TOK)
+                keep = key >= start
+                if b == t:
+                    row = lax.broadcasted_iota(jnp.int32, (QROWS, TOK), 0)
+                    keep = keep & (key <= lax.rem(row, TOK) + (t * CHUNK + me.x * TOK))
+                kept.append(jnp.where(keep, score[:, b * TOK : (b + 1) * TOK], -jnp.inf))
+            score = jnp.concatenate(kept, axis=1) if t else kept[0]
+            old = top[t]
+            new = jnp.maximum(old, jnp.max(score, axis=1, keepdims=True))
+            p = jnp.exp2(score - new)
+            factor = jnp.exp2(old - new)
+            top[t] = new
+            total[t] = total[t] * factor + jnp.sum(p, axis=1, keepdims=True)
+            acc[t] = acc[t] * factor + mm(p.astype(BF), keyv[:n])
+
+    def after_own():
+        kvs.forward()
+        down_x.forward()
+
+    def before_last():
+        gu_z.forward()
+        o_z.forward()
+        cots.forward()
+        cot_sib.extend(
+            send(cot_all.at[me.rank(k, c)], cot_all.at[me.rank(k, c)], me.sibling())
+            for k in (-1, 1)
+        )
+        kvs.end()
+
+    source(0)
+    after_own()
+    pl.loop(1, 3)(source)
+    before_last()
+    source(3)
+
+    o_z.end()
+    o_x = Gather(
+        send,
+        me.along_x,
+        lambda k: o_w.at[
+            :, :, c, :, pl.ds(pl.multiple_of(me.x_at(k) * (CHUNK * 3 // 4), TOK), CHUNK * 3 // 4)
+        ],
+        halves,
+    )
+    kv_copy = send.local(kv, kv_out)
+    bits = []
+    for t in range(NT):
+        o = acc[t][:, HD : 2 * HD] / total[t]
+        lse = top[t] + jnp.log2(total[t])
+        o_out[t] = o
+        lse_out[t] = jnp.transpose(jnp.broadcast_to(lse, (QROWS, TOK)))[:1]
+        place = places_of(me, t, (TOK, 2 * HD), 0)
+        _, end = starts_of(lengths, place)
+        ob = jnp.concatenate([o[:TOK], o[TOK:]], axis=1)
+        ob = jnp.where(place < end, ob, 0.0).astype(BF)
+        ob_out[t * TOK : (t + 1) * TOK] = ob[:, :TOK]
+        bits.append(ob[:, TOK:])
+    for t in range(4):
+        at = GROUP_ROWS + t * TOK
+        ob_out[at : at + TOK] = jnp.concatenate([bits[t], bits[t + 4]], axis=1)
+    down_x.end()
+    gu_z.end()
+    cots.end()
+    far = cot_all.at[me.rank(2, c)]
+    cot_sib.append(send(far, far, me.sibling()))
+    o_x.forward()
+    o_x.end()
+    send(o_w.at[:, :, c], o_w.at[:, :, c], me.sibling())
+    for copy in (own_cot, tok_out, h1_copy, kv_copy):
+        copy.wait()
+    send.finish()
+
+
+def front(lengths, tok, cot, wq, wk, wv, wg, wu, wo, wd, gain1, gain2):
+    def like(*shape, dtype=BF):
+        return jax.ShapeDtypeStruct(shape, dtype)
+
+    rows, width = wq.shape
+    part = wg.shape[1] // NT
+    freq = jnp.asarray(np.tile(frequency_table(HD), 2)[None])
+    outs = (
+        (like(NT, TOK, width), ANY),
+        (like(NT, TOK, width), ANY),
+        (like(NT, TOK, width), ANY),
+        (like(4, 4, rows, 2 * part), ANY),
+        (like(4, 2, 2, rows, width), ANY),
+        (like(4, TOK, width), ANY),
+        (like(NX, PACKED, TOK), ANY),
+        (like(NT, QROWS, TOK), VM),
+        (like(NT, QROWS, HD, dtype=F32), VM),
+        (like(NT, 1, QROWS, dtype=F32), VM),
+        (like(PACKED, TOK), VM),
+        (like(2, width, dtype=F32), VM),
+        (like(width, 4 * HD), VM),
+    )
+    padded = rows + 16
+    return pl.pallas_call(
+        front_kernel,
+        out_shape=tuple(o[0] for o in outs),
+        in_specs=[SM, VM, ANY, ANY, VM, VM, VM, VM, VM, ANY, ANY, VM, VM],
+        out_specs=tuple(o[1] for o in outs),
+        scratch_shapes=[
+            pltpu.VMEM((NT, TOK, width), BF),
+            pltpu.VMEM((NT, TOK, width), BF),
+            pltpu.VMEM((NT, padded, 4 * HD), BF),
+            pltpu.VMEM((NT, rows, 2 * part), BF),
+            pltpu.VMEM((padded, 4 * HD), BF),
+            pltpu.VMEM((rows, 2 * part), BF),
+            pltpu.VMEM((4, 4, padded, 4 * HD), BF),
+            pltpu.VMEM((NX, PACKED, TOK), BF),
+            pltpu.VMEM((GROUP_ROWS, 2 * TOK), BF),
+            pltpu.VMEM((NT, TOK, TOK), jnp.int32),
+            pltpu.VMEM((NT, QROWS, 1), F32),
+            pltpu.VMEM((NT, QROWS, 1), F32),
+            pltpu.VMEM((NT, QROWS, 2 * TOK), F32),
+            pltpu.SemaphoreType.DMA((64,)),
+            pltpu.SemaphoreType.DMA((64,)),
+            pltpu.SemaphoreType.DMA((16,)),
+        ],
+        compiler_params=pltpu.CompilerParams(
+            collective_id=0, has_side_effects=True, vmem_limit_bytes=56 * 2**20
+        ),
+        name="front",
+    )(lengths, freq, tok, cot, wq, wk, wv, wg, wu, wo, wd, gain1, gain2)
+
+
 def gather_begin(me, send, own, out):
     return [
-        send(own, out.at[me.t], me.ring(1)),
-        send(own, out.at[me.t], me.ring(-1)),
+        send(own, out.at[me.t], me.along_y(1)),
+        send(own, out.at[me.t], me.along_y(-1)),
         send(own, out.at[me.t], me.sibling()),
     ]
 
@@ -142,11 +501,11 @@
     below, above, far = me.rank(-1, me.c), me.rank(1, me.c), me.rank(2, me.c)
     down.wait_recv()
     part = out.at[below, pl.ds(0, half)]
-    on_down = send(part, part, me.ring(1))
+    on_down = send(part, part, me.along_y(1))
     sib_below = send(out.at[below], out.at[below], me.sibling())
     up.wait_recv()
     part = out.at[above, pl.ds(half, half)]
-    on_up = send(part, part, me.ring(-1))
+    on_up = send(part, part, me.along_y(-1))
     sib_above = send(out.at[above], out.at[above], me.sibling())
     on_down.wait_recv()
     on_up.wait_recv()
@@ -165,9 +524,6 @@
     gather_rest(me, send, out, begun)
     local.wait()
     send.finish()
-
-
-ANY = pl.BlockSpec(memory_space=pl.ANY)
 
 
 def gather_group(own, name, number):
@@ -203,29 +559,26 @@
 
     from_sib[2].wait_recv()
     mid[2] = both(2, slice(None)).astype(BF)
-    far_up = send(mid.at[2, lo], far_a, me.ring(1))
-    far_down = send(mid.at[2, hi], far_b, me.ring(-1))
+    far_up = send(mid.at[2, lo], far_a, me.along_y(1))
+    far_down = send(mid.at[2, hi], far_b, me.along_y(-1))
     from_sib[1].wait_recv()
     mid[1, half:] = both(1, slice(half, TOK)).astype(BF)
-    up_hi = send(mid.at[1, hi], near_a.at[hi], me.ring(1))
+    up_hi = send(mid.at[1, hi], near_a.at[hi], me.along_y(1))
     from_sib[3].wait_recv()
     mid[3, :half] = both(3, slice(0, half)).astype(BF)
-    down_lo = send(mid.at[3, lo], near_b.at[lo], me.ring(-1))
+    down_lo = send(mid.at[3, lo], near_b.at[lo], me.along_y(-1))
     far_up.wait_recv()
     mid[1, :half] = (both(1, slice(0, half)) + far_a[...].astype(F32)).astype(BF)
-    up_lo = send(mid.at[1, lo], near_a.at[lo], me.ring(1))
+    up_lo = send(mid.at[1, lo], near_a.at[lo], me.along_y(1))
     far_down.wait_recv()
     mid[3, half:] = (both(3, slice(half, TOK)) + far_b[...].astype(F32)).astype(BF)
-    down_hi = send(mid.at[3, hi], near_b.at[hi], me.ring(-1))
+    down_hi = send(mid.at[3, hi], near_b.at[hi], me.along_y(-1))
     from_sib[0].wait_recv()
     total = both(0, slice(None))
     for copy in (up_hi, up_lo, down_lo, down_hi):
         copy.wait_recv()
     out[...] = total + near_a[...].astype(F32) + near_b[...].astype(F32)
     send.finish()
-
-
-VM = pl.BlockSpec(memory_space=pltpu.VMEM)
 
 
 def scatter_group(part, name, number):
@@ -253,133 +606,8 @@
     )(part)
 
 
-def first_kernel(
-    tok, wqkv, wgu, wo, tok_all, qkv, gu, oh, tmp_qkv, tmp_gu, send_sem, recv_sem, local_sem
-):
-    me = Place()
-    me.greet()
-    send = Copies(send_sem, recv_sem)
-    c, other = me.c, 1 - me.c
-    step = 1 - 2 * c
-    slot, slot_other = me.yl * 2 + c, me.yl * 2 + other
-    toward, away = me.ring(step), me.ring(-step)
-    t_toward, t_relay, t_sib = me.rank(step, c), me.rank(step, other), me.rank(0, other)
-    pairs = ((wqkv, qkv, tmp_qkv), (wgu, gu, tmp_gu))
-    kept = []
-
-    def keep(src, dst):
-        copy = pltpu.make_async_copy(src, dst, local_sem.at[len(kept)])
-        copy.start()
-        kept.append(copy)
-
-    relays = [send(src.at[t_relay], tmp, me.sibling()) for src, _, tmp in pairs]
-    for src, dst, _ in pairs:
-        send(src.at[t_sib], dst.at[slot], me.sibling())
-        send(src.at[t_toward], dst.at[slot], toward)
-    send(wo, oh.at[me.yl], toward)
-    begun = gather_begin(me, send, tok, tok_all)
-    keep(tok, tok_all.at[me.t])
-    keep(wo, oh.at[me.yl])
-    for src, dst, _ in pairs:
-        keep(src.at[me.t], dst.at[slot])
-    for relay, (_, dst, tmp) in zip(relays, pairs):
-        relay.wait_recv()
-        send(tmp, dst.at[slot_other], away)
-    gather_rest(me, send, tok_all, begun)
-    for copy in kept:
-        copy.wait()
-    send.finish()
-
-
-def first_gather(tok, wqkv, wgu, wo):
-    def like(shape):
-        return jax.ShapeDtypeStruct(shape, BF)
-
-    rows = wo.shape[0]
-    return pl.pallas_call(
-        first_kernel,
-        out_shape=(
-            like((NT,) + tok.shape),
-            like((4,) + wqkv.shape[1:]),
-            like((4,) + wgu.shape[1:]),
-            like((2,) + wo.shape),
-            like(wqkv.shape[1:]),
-            like(wgu.shape[1:]),
-        ),
-        in_specs=[ANY] * 4,
-        out_specs=(ANY,) * 6,
-        scratch_shapes=[
-            pltpu.SemaphoreType.DMA((20,)),
-            pltpu.SemaphoreType.DMA((20,)),
-            pltpu.SemaphoreType.DMA((4,)),
-        ],
-        compiler_params=pltpu.CompilerParams(collective_id=0, has_side_effects=True),
-        name="first_gather",
-    )(tok, wqkv, wgu, wo)[:4]
-
-
-QROWS = 2 * TOK
-CHUNK = NX * TOK
-
-
 def keys_of(ref, kt):
     return jnp.concatenate([ref[x, kt] for x in range(NX)], axis=0)
-
-
-def attend_kernel(x_ref, q_ref, k_ref, v_ref, start_ref, o_ref, lse_ref):
-    x = x_ref[0]
-
-    def tile(t, kt, q, start, carry, diagonal):
-        top, total, acc = carry
-        s = mm_nt(q, keys_of(k_ref, kt))
-        place = kt * CHUNK + lax.broadcasted_iota(jnp.int32, (QROWS, CHUNK), 1)
-        keep = place >= start
-        if diagonal:
-            row = lax.broadcasted_iota(jnp.int32, (QROWS, CHUNK), 0)
-            query = t * CHUNK + x * TOK + lax.rem(row, TOK)
-            keep = keep & (place <= query)
-        s = jnp.where(keep, s, -jnp.inf)
-        new_top = jnp.maximum(top, jnp.max(s, axis=1, keepdims=True))
-        p = jnp.exp2(s - new_top)
-        factor = jnp.exp2(top - new_top)
-        total = total * factor + jnp.sum(p, axis=1, keepdims=True)
-        acc = acc * factor + mm(p.astype(BF), keys_of(v_ref, kt))
-        return new_top, total, acc
-
-    def one(t, _):
-        q = jnp.concatenate([q_ref[0, t], q_ref[1, t]], axis=0)
-        start = jnp.concatenate([start_ref[t]] * 2, axis=0)
-        carry = (
-            jnp.full((QROWS, 1), -1e30, F32),
-            jnp.zeros((QROWS, 1), F32),
-            jnp.zeros((QROWS, HD), F32),
-        )
-        carry = lax.fori_loop(0, t, lambda kt, c: tile(t, kt, q, start, c, False), carry)
-        top, total, acc = tile(t, t, q, start, carry, True)
-        o = acc / total
-        lse = top + jnp.log2(total)
-        o_ref[0, t], o_ref[1, t] = o[:TOK], o[TOK:]
-        lse_ref[0, t], lse_ref[1, t] = lse[:TOK], lse[TOK:]
-        return 0
-
-    lax.fori_loop(0, NT, one, 0)
-
-
-SM = pl.BlockSpec(memory_space=pltpu.SMEM)
-
-
-def attend(x_index, q, k, v, start):
-    return pl.pallas_call(
-        attend_kernel,
-        out_shape=(
-            jax.ShapeDtypeStruct((2, NT, TOK, HD), F32),
-            jax.ShapeDtypeStruct((2, NT, TOK, 1), F32),
-        ),
-        in_specs=[SM, VM, VM, VM, VM],
-        out_specs=(VM, VM),
-        compiler_params=pltpu.CompilerParams(vmem_limit_bytes=40 * 2**20),
-        name="attend",
-    )(x_index, q, k, v, start)
 
 
 def attend_back_kernel(
@@ -441,7 +669,7 @@
     )(x_index, q, k, v, go, start, lse, delta)
 
 
-def turn(v, cosine, sine):
+def turn3(v, cosine, sine):
     half = HD // 2
     v1, v2 = v[..., :half], v[..., half:]
     return jnp.concatenate([v1 * cosine - v2 * sine, v2 * cosine + v1 * sine], axis=-1)
@@ -471,31 +699,26 @@
     ylc = yl * 2 + c
     x_scalar = x_index.reshape(1)
 
-    wqkv = jnp.concatenate(
-        [
-            w_query.reshape(rows, NT, 2 * HD),
-            w_key.reshape(rows, NT, HD),
-            w_value.reshape(rows, NT, HD),
-        ],
-        axis=2,
-    ).transpose(1, 0, 2)
-
-    def hidden_slices(w):
-        w = w.reshape(rows, 4, 4, 2, TOK).transpose(2, 3, 0, 1, 4)
-        return w.reshape(NT, rows, part)
-
-    wgu = jnp.concatenate([hidden_slices(w_gate), hidden_slices(w_up)], axis=2)
-    down_own = lax.dynamic_slice_in_dim(w_down, yh * TOK, TOK, 0)
-    gains = lax.all_gather(jnp.stack([gain_attn, gain_mlp], axis=1), everyone, axis=0, tiled=True)
-    gains = gains.astype(F32)
-    g1, g2 = gains[:, 0][None, :], gains[:, 1][None, :]
-    tok_all, qkv_part, gu_part, o_half = first_gather(tokens[0], wqkv, wgu, w_output)
-    qkv_w = lax.all_gather(qkv_part, "z", axis=0, tiled=True).reshape(width, 4 * HD)
-    gu_w = lax.all_gather(gu_part, "z", axis=0, tiled=True).reshape(width, 2 * part)
-    down_w = lax.all_gather(down_own, "z", axis=0, tiled=True)
-    o_w = lax.all_gather(o_half, ("z", "c"), axis=0)
-    o_w = o_w.reshape((4, 2) + o_half.shape).transpose(0, 2, 1, 3, 4).reshape(width, width)
-    cot_all = lax.all_gather(cotangent[0], GROUP, axis=0, tiled=True)
+    tok_all, cot_all, h1, gu_w, o_w, down_w, kv_packed, qp, o, lse, ob, gains, qkv_w = front(
+        doc_lengths,
+        tokens[0],
+        cotangent[0],
+        w_query,
+        w_key,
+        w_value,
+        w_gate,
+        w_up,
+        w_output,
+        w_down,
+        gain_attn.reshape(1, -1),
+        gain_mlp.reshape(1, -1),
+    )
+    gu_w = gu_w.reshape(width, 2 * part)
+    o_w = o_w.reshape(width, width)
+    down_w = down_w.reshape(part, width)
+    cot_all = cot_all.reshape(NT * TOK, width)
+    h1 = h1.reshape(NT * TOK, width)
+    g1, g2 = gains[:1], gains[1:]
 
     lengths = doc_lengths[0]
     places = (
@@ -510,19 +733,14 @@
     start = start.reshape(NT, TOK)
 
     x_all = tok_all.reshape(NT * TOK, width).astype(F32)
-    h1 = x_all * lax.rsqrt(jnp.mean(x_all * x_all, axis=1, keepdims=True) + NORM_EPS)
-    h1 = (h1 * g1).astype(BF)
-    qkv = mm(h1, qkv_w)
-    q = turn(qkv[:, : 2 * HD].reshape(-1, 2, HD), cosine[:, None], sine[:, None])
-    q = (q * (SCALE * LOG2E)).astype(BF).transpose(1, 0, 2).reshape(2, NT, TOK, HD)
-    k = turn(qkv[:, 2 * HD : 3 * HD], cosine, sine).astype(BF).reshape(NT, TOK, HD)
-    v = qkv[:, 3 * HD :].astype(BF).reshape(NT, TOK, HD)
-    kv = lax.all_gather(jnp.stack([k, v]), "x", axis=0)
-    k_all, v_all = kv[:, 0], kv[:, 1]
-    attended, lse = attend(x_scalar, q, k_all, v_all, start[..., None])
-    flat = attended.transpose(1, 2, 0, 3).reshape(NT * TOK, 2 * HD)
-    ob = (flat * valid).astype(BF)
+    q = qp[:, :, :HD].reshape(NT, 2, TOK, HD).transpose(1, 0, 2, 3)
+    kv_all = jax.vmap(lambda a: unpack(a, NT * TOK))(kv_packed)
+    k_all = kv_all[:, :, :HD].reshape(NX, NT, TOK, HD)
+    v_all = kv_all[:, :, HD : 2 * HD].reshape(NX, NT, TOK, HD)
+    flat = o.reshape(NT, 2, TOK, HD).transpose(0, 2, 1, 3).reshape(NT * TOK, 2 * HD)
+    lse = lse.reshape(NT, 2, TOK).transpose(1, 0, 2)[:, :, None, :]
     ob_all = gather_group(ob, "gather_ob", 1)
+    ob_all = jax.vmap(lambda a: unpack(a, NT * TOK))(ob_all)[:, :, : 2 * HD]
     ob_all = ob_all.transpose(1, 0, 2).reshape(NT * TOK, width)
 
     x2 = x_all + mm(ob_all, o_w)
@@ -556,12 +774,12 @@
     delta = delta.transpose(2, 0, 1)[:, :, None, :]
     go4 = go.reshape(NT, TOK, 2, HD).transpose(2, 0, 1, 3)
     gq, gk, gv = attend_back(
-        x_scalar, q, k_all, v_all, go4, start[:, None, :], lse.transpose(0, 1, 3, 2), delta
+        x_scalar, q, k_all, v_all, go4, start[:, None, :], lse, delta
     )
     gkv = jnp.stack([gk * LN2, gv], axis=1).astype(BF)
     gkv = lax.psum_scatter(gkv, "x", scatter_dimension=0).astype(F32)
-    gq = turn(gq.transpose(1, 2, 0, 3).reshape(-1, 2, HD), cosine[:, None], -sine[:, None])
-    gk = turn(gkv[0].reshape(-1, HD), cosine, -sine)
+    gq = turn3(gq.transpose(1, 2, 0, 3).reshape(-1, 2, HD), cosine[:, None], -sine[:, None])
+    gk = turn3(gkv[0].reshape(-1, HD), cosine, -sine)
     gqkv = jnp.concatenate([gq.reshape(-1, 2 * HD), gk, gkv[1].reshape(-1, HD)], axis=1).astype(BF)
     gh1_part = mm_nt(gqkv, qkv_w).astype(BF).reshape(NT, TOK, width)
     gh1 = scatter_group(gh1_part, "scatter_gh1", 5)

time: 707 us -> 574 us (0.81)
  waiting for transfers between devices: 258 us -> 139 us
  Pallas kernels: 207 us -> 253 us
  local copies, waits for them, and re-layouts: 73.4 us -> 50.8 us
  blocking collectives: 34.2 us -> 15.2 us
  other arithmetic: 42.4 us -> 31 us
  matrix products: 62.1 us -> 54.4 us
    all_gather x6 -> x0, waiting for transfers between devices: 118 us -> none  [the longest x1 74.4 us: body(): cot_all = lax.all_gather(cotangent[0], GROUP, axis=0, tiled=True)]
    pallas_call x2 -> x1, Pallas kernels: 49 us -> 102 us  [front(): pl.pallas_call(front_kernel, out_shape=tuple((o[0] for o in outs)), in_sp...]
    all_gather x1 -> x0, blocking collectives: 19 us -> none  [body(): lax.all_gather(jnp.stack([gain_attn, gain_mlp], axis=1), everyone, axis=0...]
    reshape x13 -> x1, local copies, waits for them, and re-layouts: 12 us -> 0.83 us  [body(): q = qp[:, :, :HD].reshape(NT, 2, TOK, HD).transpose(1, 0, 2, 3)]
    convert_element_type x4 -> x0, other arithmetic: 9.21 us -> none  [the longest x2 6.96 us: body(): h1 = (h1 * g1).astype(BF)]
    unnamed x77 -> x54, local copies, waits for them, and re-layouts: 15.3 us -> 7.6 us
    dot_general x4 -> x3, matrix products: 24.1 us -> 21.7 us  [mm(): return jnp.dot(a, b, preferred_element_type=F32)]
  transfers between devices with their start and end apart: 14 -> 8, of which waited for: 11 -> 6; matrix products, arithmetic and copies ran while one was open for 14% -> 8% of each run, Pallas kernels for 16% -> 12%
where the time goes in v2:
time: 574 us; the launch traced here: 565 us
  Pallas kernels  253 us (44%)
  waiting for transfers between devices  139 us (24%)
  matrix products  54.4 us (9%)
  local copies, waits for them, and re-layouts  50.8 us (9%)
  other arithmetic  31 us (5%)
  blocking collectives  15.2 us (3%)
  between operations  15.1 us (3%)
  starting transfers between devices  5.83 us (1%)
    pallas_call x1, Pallas kernels, front(): pl.pallas_call(front_kernel, out_shape=tuple((o[0] for o in outs)), in_sp...  102 us
    pallas_call x3, Pallas kernels, scatter_group(): pl.pallas_call(scatter_kernel, out_shape=jax.ShapeDtypeStruct((rows, widt...  87.2 us
    reduce_scatter x4, waiting for transfers between devices, over_z(): return lax.psum_scatter(a, 'z', scatter_dimension=0, tiled=True)  76 us
    psum x1, waiting for transfers between devices, body(): columns, sum_down, sum_o = lax.psum((columns, sum_down, sum_o), 'x')  54 us
    pallas_call x2, Pallas kernels, gather_group(): pl.pallas_call(gather_kernel, out_shape=jax.ShapeDtypeStruct((NT, rows, w...  41 us
    pallas_call x1, Pallas kernels, attend_back(): pl.pallas_call(attend_back_kernel, out_shape=(jax.ShapeDtypeStruct((2, NT...  22.7 us
    dot_general x3, matrix products, mm(): return jnp.dot(a, b, preferred_element_type=F32)  21.7 us
    dot_general x4, matrix products, mm_tn(): lax.dot_general(a, b, (((0,), (0,)), ((), ())), preferred_element_type=F32)  20.2 us
  transfers between devices with their start and end apart: 8, of which 6 were waited for; matrix products, arithmetic and copies ran while one was open for 8% of the time, Pallas kernels for 12%

profile of v2, /device:TPU:27, one launch (start us, length us, event | category | flops | bytes accessed | tf_op | source)
XLA Modules:
  0.0 565.0 jit_solution(13717404023461513635)
XLA Ops:
  9.3 102.2 %front.1 = (bf16[8,128,1536]{2,1,0:T(8,128)(2,1)}, bf16[8,128,1536]{2,1,0:T(8,128)(2,1)}, bf16[8,128,1536]{2,1,0:T(8,128)(2,1)}, bf16[4,4,96,1024]{3,2,1,0:T(8,1...) custom-call(s32[1,8]{1,0:T(1,128)} %lengths.1, ...), custom_call_target="tpu_custom_call" | custom-call | tf_op jit(solution)/shard_map/front/pallas_call | solution.py:460
  114.5 20.0 %gather_ob.1 = bf16[8,1536,128]{2,1,0:T(8,128)(2,1)} custom-call(bf16[1536,128]{1,0:T(8,128)(2,1)} %get-tuple-element.28.own), custom_call_target="tpu_custom_call" | custom-call | tf_op jit(solution)/shard_map/gather_ob/pallas_call | solution.py:531
  134.5 3.2 slice.90
  140.6 2.5 copy.113
  143.1 3.9 maximum_bitcast_fusion
  147.0 6.2 %copy.108 = bf16[1024,8,192]{0,2,1:T(8,128)(2,1)} copy(bf16[1024,8,192]{2,0,1:T(8,128)(2,1)} %maximum_bitcast_fusion) | data formatting | bytes 6291456 | tf_op jit(solution)/shard_map/transpose | solution.py:744
  153.2 11.0 %multiply_reduce_fusion = (f32[1024]{0:T(1024)S(1)}, f32[1024,1536]{1,0:T(8,128)}) fusion(bf16[1024,1536]{0,1:T(8,128)(2,1)} %bitcast.154, bf16[1536,1536]{1,0:T(8,128)(2,1)} %bitcast.179, bf16[1024,1536]{1,0:T(8,128)(2,1)} %bitcast.186), kind=kOutput, calls=%fused_computation.2 | convolution fusion | flops 4838128640 | bytes 17305600 | tf_op jit(solution)/shard_map/dot_general | solution.py:54
  164.3 7.1 %fusion.33 = f32[1024,1024]{0,1:T(8,128)S(1)} fusion(bf16[1536,1024]{1,0:T(8,128)(2,1)} %bitcast.184, f32[1024,1536]{1,0:T(8,128)} %get-tuple-element.82, f32[1536]{0:T(1024)S(1)} %get-tuple-element.50, f32[1024]{0:T(1024)S(1)} %add_rsqrt_fusion), kind=kOutput, calls=%fused_computation.95 | convolution fusion | flops 3225944064 | bytes 13641728 | tf_op jit(solution)/shard_map/dot_general | solution.py:54
  171.5 3.5 multiply_convert_fusion.3
  175.0 3.9 convolution_convert_fusion.3
  178.9 18.4 %scatter_gh2.1 = f32[128,1536]{1,0:T(8,128)S(1)} custom-call(bf16[8,128,1536]{2,1,0:T(8,128)(2,1)S(1)} %bitcast.144), custom_call_target="tpu_custom_call" | custom-call | tf_op jit(solution)/shard_map/scatter_gh2/pallas_call | solution.py:587
  201.0 21.0 %gather_ga.1 = bf16[8,128,1536]{2,1,0:T(8,128)(2,1)} custom-call(bf16[128,1536]{1,0:T(8,128)(2,1)} %fusion.32.own), custom_call_target="tpu_custom_call" | custom-call | tf_op jit(solution)/shard_map/gather_ga/pallas_call | solution.py:531
  222.0 3.3 fusion.8
  233.6 22.7 %attend_back.1 = (f32[2,8,128,96]{3,2,1,0:T(8,128)S(1)}, f32[4,8,128,96]{3,2,1,0:T(8,128)}, f32[4,8,128,96]{3,2,1,0:T(8,128)}) custom-call(s32[1]{0:T(128)} %bitcast.14.x_ref, bf16[2,8,128,96]{3,2,1,0:T(8,128)(2,1)S(1)} %bitcast.147, bf16[4,8,128,96]{3,2,1,0:T(8,128)(2,1)S(1)} %bitcast.142, bf16[4,8,128,96]{3,2,1,0:T(8,128)(2,1)S(1)} %bitcast.141, ...), custom_call_target="tpu_custom_call" | custom-call | tf_op jit(solution)/shard_map/attend_back/pallas_call | solution.py:658
  256.3 2.7 fusion.9
  260.8 4.0 copy.116
  264.9 8.5 %convolution_convert_fusion.2 = bf16[1536,1024]{1,0:T(8,128)(2,1)} fusion(bf16[1024,512]{0,1:T(8,128)(2,1)} %copy-done.23, bf16[1024,512]{0,1:T(8,128)(2,1)S(1)} %copy-done.22, f32[1024,1536]{1,0:T(8,128)} %get-tuple-element.82, f32[1536]{0:T(1024)S(1)} %get-tuple-element.50, f32[1024]{0:T(1024)S(1)} %add_rsqrt_fusion), kind=kOutput, calls=%fused_computation.7 | convolution fusion | flops 3231711232 | bytes 11544576 | tf_op jit(solution)/shard_map/dot_general | solution.py:62
  278.6 9.3 %reduce-scatter.6.cloned.1.call-done = bf16[1,2,8,128,96]{3,4,2,1,0:T(8,128)(2,1)} async-done(((bf16[4,2,8,128,96]{3,4,2,1,0:T(8,128)(2,1)}), bf16[1,2,8,128,96]{3,4,2,1,0:T(8,128)(2,1)}) %reduce-scatter.6.cloned.1.call-update) | async-done | bytes 393232 | tf_op jit(solution)/shard_map/reduce_scatter | solution.py:780
  292.3 19.1 %scatter_gh1.1 = f32[128,1536]{1,0:T(8,128)S(1)} custom-call(bf16[8,128,1536]{2,1,0:T(8,128)(2,1)S(1)} %bitcast.145), custom_call_target="tpu_custom_call" | custom-call | tf_op jit(solution)/shard_map/scatter_gh1/pallas_call | solution.py:587
  312.0 3.8 convolution_convert_fusion.5
  318.4 3.1 fusion.5
  321.6 4.8 convolution_convert_fusion.4
  326.5 3.6 reduce-scatter.8.cloned.1.call-done
  330.0 27.7 %reduce-scatter.10.cloned.1.call-done = bf16[384,512]{1,0:T(8,128)(2,1)} async-done(((bf16[1536,512]{1,0:T(8,128)(2,1)}), bf16[384,512]{1,0:T(8,128)(2,1)}) %reduce-scatter.10.cloned.1.call-update) | async-done | bytes 393232 | tf_op jit(solution)/shard_map/reduce_scatter | solution.py:804
  360.1 5.4 all-to-all-start
  365.4 15.6 %reduce-scatter.12.cloned.1.call-done = bf16[96,768]{1,0:T(8,128)(2,1)} async-done(((bf16[384,768]{1,0:T(8,128)(2,1)}), bf16[96,768]{1,0:T(8,128)(2,1)}) %reduce-scatter.12.cloned.1.call-update) | async-done | bytes 147472 | tf_op jit(solution)/shard_map/reduce_scatter | solution.py:804
  381.0 29.2 %reduce-scatter.14.cloned.1.call-done = bf16[128,1536]{1,0:T(8,128)(2,1)} async-done(((bf16[512,1536]{1,0:T(8,128)(2,1)}), bf16[128,1536]{1,0:T(8,128)(2,1)}) %reduce-scatter.14.cloned.1.call-update) | async-done | bytes 393232 | tf_op jit(solution)/shard_map/reduce_scatter | solution.py:804
  411.3 54.0 %all-reduce.4.cloned.1.call-done = (bf16[1,384,1536]{2,1,0:T(8,128)(2,1)}, bf16[96,768]{1,0:T(8,128)(2,1)}, bf16[128,1536]{1,0:T(8,128)(2,1)}) async-done(((bf16[1,384,1536]{2,1,0:T(8,128)(2,1)}, bf16[96,768]{1,0:T(8,128)(2,1)}, bf16[128,1536]{1,0:T(8,128)(2,1)}), (bf16[1,384,1536]{2,1,0:T(8,128)(2,1)}, bf16[96,768]{1,0:T(8,128)(2,1)}, bf16[128,1536]{1,0:T(8,128)(2,1)})) %all-reduce.4.cloned.1.call-update) | async-done | bytes 1720336 | tf_op jit(solution)/shard_map/psum | solution.py:810
  465.4 3.6 convolution_convert_fusion.1
  469.0 49.7 %scatter_y.1 = f32[128,1536]{1,0:T(8,128)S(1)} custom-call(bf16[8,128,1536]{2,1,0:T(8,128)(2,1)S(1)} %bitcast.143), custom_call_target="tpu_custom_call" | custom-call | tf_op jit(solution)/shard_map/scatter_y/pallas_call | solution.py:587
  521.2 6.2 %all_gather.14 = bf16[96,1536]{1,0:T(8,128)(2,1)S(1)} all-gather(bf16[96,768]{1,0:T(8,128)(2,1)S(1)} %copy-done.12), channel_id=1, replica_groups=mesh['z'=4,'yl'=2,'c'=2,'yh'=2,'x'=4] {'yh'}, dimensions={1}, use_global_device_ids=true | all-gather | bytes 442368 | tf_op jit(solution)/shard_map/all_gather | solution.py:813
  528.2 9.0 %all_gather.15 = bf16[256,1536]{1,0:T(8,128)(2,1)S(1)} all-gather(bf16[128,1536]{1,0:T(8,128)(2,1)S(1)} %copy-done.11), channel_id=1, replica_groups=mesh['z'=4,'yl'=2,'c'=2,'yh'=2,'x'=4] {'yh'}, dimensions={0}, use_global_device_ids=true | all-gather | bytes 1179648 | tf_op jit(solution)/shard_map/all_gather | solution.py:812
  (136 shorter events, 61.8 us)
Async XLA Ops:
  7.2 280.7 %reduce-scatter.6.cloned.1.call-start = ((), (), s32[]{:S(2)}) async-start(), calls=%async_computation.6 | async-start | bytes 1966080 | tf_op jit(solution)/shard_map/reduce_scatter | solution.py:780
  111.6 1.7 copy-start.4
  134.5 3.2 copy-start.1
  137.7 2.0 copy-start.14
  137.8 2.0 copy-start.13
  137.8 2.1 copy-start.10
  164.3 7.1 %copy-start.16 = (bf16[8,128,1536]{2,1,0:T(8,128)(2,1)S(1)}, bf16[8,128,1536]{2,1,0:T(8,128)(2,1)}, u32[]{:S(2)}) copy-start(bf16[8,128,1536]{2,1,0:T(8,128)(2,1)} %get-tuple-element.33) | copy-start | bytes 9437188
  164.3 7.1 %copy-start.18 = (bf16[4,128,1536]{2,1,0:T(8,128)(2,1)S(1)}, bf16[4,128,1536]{2,1,0:T(8,128)(2,1)}, u32[]{:S(2)}) copy-start(bf16[4,128,1536]{2,1,0:T(8,128)(2,1)} %get-tuple-element.32) | copy-start | bytes 4718596
  171.5 3.5 copy-start.17
  175.0 3.9 copy-start.21
  175.0 3.9 copy-start.23
  178.9 19.9 %copy-start.6 = (bf16[1,128,1536]{2,1,0:T(8,128)(2,1)S(1)}, bf16[1,128,1536]{2,1,0:T(8,128)(2,1)}, u32[]{:S(2)}) copy-start(bf16[1,128,1536]{2,1,0:T(8,128)(2,1)} %param.25) | copy-start | bytes 1179652
  222.0 3.3 copy-start.8
  232.5 1.0 copy-start
  260.8 4.1 copy-start.22
  264.8 65.2 %reduce-scatter.8.cloned.1.call-start = ((), (), s32[]{:S(2)}) async-start(), calls=%async_computation.7 | async-start | bytes 3932160 | tf_op jit(solution)/shard_map/reduce_scatter | solution.py:804
  273.4 84.4 %reduce-scatter.10.cloned.1.call-start = ((), (), s32[]{:S(2)}) async-start(), calls=%async_computation.8 | async-start | bytes 1966080 | tf_op jit(solution)/shard_map/reduce_scatter | solution.py:804
  275.3 3.2 copy-start.2
  276.9 12.5 %copy-start.15 = (f32[48]{0:T(128)S(1)}, f32[48]{0:T(128)}, u32[]{:S(2)}) copy-start(f32[48]{0:T(128)} %constant.66.clone) | copy-start | bytes 580
  289.2 1.3 copy-start.19
  317.1 63.9 %reduce-scatter.12.cloned.1.call-start = ((), (), s32[]{:S(2)}) async-start(), calls=%async_computation.10 | async-start | bytes 737280 | tf_op jit(solution)/shard_map/reduce_scatter | solution.py:804
  318.4 3.2 copy-start.20
  321.6 88.6 %reduce-scatter.14.cloned.1.call-start = ((), (), s32[]{:S(2)}) async-start(), calls=%async_computation.11 | async-start | bytes 1966080 | tf_op jit(solution)/shard_map/reduce_scatter | solution.py:804
  360.1 50.2 %all-to-all-start = ((bf16[4,96,1536]{2,1,0:T(8,128)(2,1)}), bf16[4,96,1536]{2,1,0:T(8,128)(2,1)S(1)}, u32[]{:S(2)}, u32[]{:S(2)}) async-start(bf16[4,96,1536]{2,1,0:T(8,128)(2,1)} %bitcast.44), calls=%async_computation.3 | async-start | bytes 2359296 | tf_op jit(solution)/shard_map/all_to_all | solution.py:809
  365.4 99.9 %all-reduce.4.cloned.1.call-start = ((), (), s32[]{:S(2)}) async-start(), calls=%async_computation.12 | async-start | bytes 3440640 | tf_op jit(solution)/shard_map/psum | solution.py:810
  410.2 1.0 copy-start.5
  411.3 127.3 %all-gather.2.cloned.1.call-start = ((), (), s32[]{:S(2)}) async-start(), calls=%async_computation.9 | async-start | bytes 3538944 | tf_op jit(solution)/shard_map/all_gather | solution.py:811
  468.9 49.8 %copy-start.7 = (bf16[1,128,1536]{2,1,0:T(8,128)(2,1)S(1)}, bf16[1,128,1536]{2,1,0:T(8,128)(2,1)}, u32[]{:S(2)}) copy-start(bf16[1,128,1536]{2,1,0:T(8,128)(2,1)} %param.25) | copy-start | bytes 1179652
  518.7 2.5 copy-start.12
  518.7 9.5 %copy-start.11 = (bf16[128,1536]{1,0:T(8,128)(2,1)S(1)}, bf16[128,1536]{1,0:T(8,128)(2,1)}, u32[]{:S(2)}) copy-start(bf16[128,1536]{1,0:T(8,128)(2,1)} %get-tuple-element.53) | copy-start | bytes 1179652
  548.1 2.4 copy-start.9
  550.5 3.0 copy-start.3
Sparse Core Ops, SparseCore 0:
  264.9 22.9 reduce-scatter.5
  290.3 39.7 reduce-scatter.7
  333.0 24.6 reduce-scatter.9
  360.5 20.4 reduce-scatter.11
  383.9 26.3 reduce-scatter.13
  413.2 52.1 all-reduce.3
  467.1 47.3 all-gather.1
